TPU v7x, 32 devices: a whole 2x2x4 slice. The times are simulated.
32 devices in a mesh: dp: 4 (over y, core), row: 2 (over x), col: 4 (over z).
Axes of the slice: x: 2, y: 2, z: 4, core: 2. Of those that a mesh axis runs over, the one named last changes fastest.
Arguments:
- tokens: float32 [10240, 1024], P(('dp', 'row'), 'col'), may hold values from -6 to 6
- lengths: int32 [16, 4], P(('dp', 'col')), may hold values from 1 to 512, 640 in all within a row
- w_qkv: float32 [1024, 3, 1024], P('col', None, 'row'), may hold values from -0.1875 to 0.1875
- qv_bias: float32 [2, 1024], P(None, 'row'), may hold values from -3 to 3
- w_out: float32 [1024, 1024], P('row', 'col'), may hold values from -1.5 to 1.5
- out_bias: float32 [1024], P('col'), may hold values from -3 to 3
- w_up: float32 [1024, 4096], P('col', 'row'), may hold values from -0.1875 to 0.1875
- up_bias: float32 [4096], P('row'), may hold values from -3 to 3
- w_down: float32 [4096, 1024], P('row', 'col'), may hold values from -0.09375 to 0.09375
- down_bias: float32 [1024], P('col'), may hold values from -3 to 3
- norm_gain: float32 [2, 1024], P(None, 'col'), may hold values from 0.25 to 1.75
- norm_bias: float32 [2, 1024], P(None, 'col'), may hold values from -2 to 2
- cotangent: float32 [10240, 1024], P(('dp', 'row'), 'col'), may hold values from -6 to 6
Outputs:
- output: float32 [10240, 1024], P(('dp', 'row'), 'col')
- grad_input: float32 [10240, 1024], P(('dp', 'row'), 'col')
- grad_w_qkv: float32 [1024, 3, 1024], P('col', None, 'row')
- grad_qv_bias: float32 [2, 1024], P(None, 'row')
- grad_w_out: float32 [1024, 1024], P('row', 'col')
- grad_out_bias: float32 [1024], P('col')
- grad_w_up: float32 [1024, 4096], P('col', 'row')
- grad_up_bias: float32 [4096], P('row')
- grad_w_down: float32 [4096, 1024], P('row', 'col')
- grad_down_bias: float32 [1024], P('col')
- grad_norm_gain: float32 [2, 1024], P(None, 'col')
- grad_norm_bias: float32 [2, 1024], P(None, 'col')
Inputs may be any that keep to these rules, and one draw needn't show every extreme that they name: Each row lists the lengths of the 4 sequences of one data row in order; they sum to 640.
All inputs are finite; a program needn't handle non-finite values.
Results may differ from a plain program's by a relative error of at most 0.015.
The roundings to bfloat16 on the way count: a program that leaves them out, or rounds other values in their place, can miss the bound.
Values may be sent and summed in bfloat16 or wider, within the bound.
A program may use at most 192 MiB of HBM per device.

v0:
```python
from functools import partial
import math

import jax
import jax.numpy as jnp
from jax import lax
from jax.sharding import PartitionSpec as P

D = 1024
HD = 64


EPS = 1e-05


def gather_rows(values):
    return lax.all_gather(values, "row", axis=0, tiled=True)


def sum_rows(values):
    return lax.psum_scatter(values, "row", scatter_dimension=0, tiled=True)


def sum_heads(values):
    return lax.psum_scatter(values, "col", scatter_dimension=0, tiled=True)


def gather_heads(values):
    return lax.all_gather(values, "col", axis=0, tiled=True)


def sum_hidden(values):
    return lax.psum_scatter(values, "col", scatter_dimension=0, tiled=True)


def gather_hidden(values):
    return lax.all_gather(values, "col", axis=0, tiled=True)


def col_totals(first_sum, second_sum):
    return lax.psum((first_sum, second_sum), "col")


def norm_forward(values, gain_row, shift_row):
    stat_sums = col_totals(jnp.sum(values, -1), jnp.sum(values * values, -1))
    center = (stat_sums[0] / D)[:, None]
    spread = (stat_sums[1] / D)[:, None] - center * center
    inv_std = lax.rsqrt(spread + EPS)
    normal = (values - center) * inv_std
    return (normal * gain_row + shift_row, normal, inv_std)


def norm_backward(grad_out, normal, inv_std, gain_row):
    scaled = grad_out * gain_row
    stat_sums = col_totals(jnp.sum(scaled, -1), jnp.sum(scaled * normal, -1))
    return inv_std * (scaled - (stat_sums[0] / D)[:, None] - normal * (stat_sums[1] / D)[:, None])


def masked_scores(query_rows, key_rows, same_seq, score_scale):
    scores = (
        jnp.einsum("qhe,khe->hqk", query_rows, key_rows, preferred_element_type=jnp.float32)
        * score_scale
    )
    return jnp.where(same_seq, scores, -1000000000.0)


def attend(query_rows, key_rows, value_rows, same_seq, score_scale):
    scores = masked_scores(query_rows, key_rows, same_seq, score_scale)
    row_max = jnp.max(scores, -1, keepdims=True)
    exp_scores = jnp.exp(scores - row_max)
    totals = jnp.sum(exp_scores, -1, keepdims=True)
    attn_probs = (exp_scores / totals).astype(jnp.bfloat16)
    context = jnp.einsum("hqk,khe->qhe", attn_probs, value_rows, preferred_element_type=jnp.float32)
    return (context, row_max + jnp.log(totals))


def attend_back(query_rows, key_rows, value_rows, same_seq, score_scale, log_total, grad_context):
    scores = masked_scores(query_rows, key_rows, same_seq, score_scale)
    attn_probs = jnp.exp(scores - log_total)
    grad_probs = jnp.einsum(
        "qhe,khe->hqk", grad_context, value_rows, preferred_element_type=jnp.float32
    )
    grad_values = jnp.einsum(
        "hqk,qhe->khe",
        attn_probs.astype(jnp.bfloat16),
        grad_context,
        preferred_element_type=jnp.float32,
    )
    inner_sum = jnp.sum(attn_probs * grad_probs, -1, keepdims=True)
    grad_scores = (attn_probs * (grad_probs - inner_sum)).astype(jnp.bfloat16)
    grad_queries = (
        jnp.einsum("hqk,khe->qhe", grad_scores, key_rows, preferred_element_type=jnp.float32)
        * score_scale
    )
    grad_keys = (
        jnp.einsum("hqk,qhe->khe", grad_scores, query_rows, preferred_element_type=jnp.float32)
        * score_scale
    )
    return (grad_queries, grad_keys, grad_values)


def shards(
    tokens,
    lengths,
    w_qkv,
    qv_bias,
    w_out,
    out_bias,
    w_up,
    up_bias,
    w_down,
    down_bias,
    norm_gain,
    norm_bias,
    cotangent,
):
    score_scale = 1.0 / math.sqrt(HD)
    gelu_exact = partial(jax.nn.gelu, approximate=False)
    w_qkv_low = w_qkv.astype(jnp.bfloat16)
    w_out_low = w_out.astype(jnp.bfloat16)
    w_up_low = w_up.astype(jnp.bfloat16)
    w_down_low = w_down.astype(jnp.bfloat16)
    tokens_all = gather_rows(tokens.astype(jnp.bfloat16))
    qkv_part = jnp.einsum("td,dsh->tsh", tokens_all, w_qkv_low, preferred_element_type=jnp.float32)
    qkv_sum = sum_heads(qkv_part)
    full_bias = jnp.stack([qv_bias[0], jnp.zeros_like(qv_bias[0]), qv_bias[1]])
    qkv = (qkv_sum + full_bias).astype(jnp.bfloat16)
    length = qkv.shape[0]
    head_count = qkv.shape[2] // HD
    query_rows = qkv[:, 0].reshape(length, head_count, HD)
    key_rows = qkv[:, 1].reshape(length, head_count, HD)
    value_rows = qkv[:, 2].reshape(length, head_count, HD)
    seq_ends = jnp.cumsum(lengths[0])
    positions = jnp.arange(length, dtype=jnp.int32)
    segment = jnp.sum((positions[:, None] >= seq_ends[None, :]).astype(jnp.int32), -1)
    same_seq = (segment[:, None] == segment[None, :])[None]
    context, log_total = attend(query_rows, key_rows, value_rows, same_seq, score_scale)
    context_all = gather_heads(context.reshape(length, head_count * HD).astype(jnp.bfloat16))
    attn_out = (
        sum_rows(jnp.dot(context_all, w_out_low, preferred_element_type=jnp.float32)) + out_bias
    )
    normed_one, normal_one, inv_one = norm_forward(tokens + attn_out, norm_gain[0], norm_bias[0])
    normed_all = gather_rows(normed_one.astype(jnp.bfloat16))
    up_part = jnp.dot(normed_all, w_up_low, preferred_element_type=jnp.float32)
    pre_act = sum_hidden(up_part) + up_bias
    hidden_all = gather_hidden(gelu_exact(pre_act).astype(jnp.bfloat16))
    mlp_out = (
        sum_rows(jnp.dot(hidden_all, w_down_low, preferred_element_type=jnp.float32)) + down_bias
    )
    output, normal_two, inv_two = norm_forward(normed_one + mlp_out, norm_gain[1], norm_bias[1])
    grad_last = norm_backward(cotangent, normal_two, inv_two, norm_gain[1])
    gain_two = jnp.sum(cotangent * normal_two, 0)
    shift_two = jnp.sum(cotangent, 0)
    grad_mlp_all = gather_rows(grad_last.astype(jnp.bfloat16))
    grad_down_bias = jnp.sum(grad_mlp_all, 0, dtype=jnp.float32)
    grad_w_down = jnp.einsum(
        "tf,td->fd", hidden_all, grad_mlp_all, preferred_element_type=jnp.float32
    )
    hidden_part = jnp.einsum(
        "td,fd->tf", grad_mlp_all, w_down_low, preferred_element_type=jnp.float32
    )
    grad_hidden = sum_hidden(hidden_part)
    gelu_pull = jax.vjp(gelu_exact, pre_act)[1]
    grad_pre_all = gather_hidden(gelu_pull(grad_hidden)[0].astype(jnp.bfloat16))
    grad_up_bias = jnp.sum(grad_pre_all, 0, dtype=jnp.float32)
    grad_w_up = jnp.einsum(
        "td,tf->df", normed_all, grad_pre_all, preferred_element_type=jnp.float32
    )
    grad_normed = (
        sum_rows(
            jnp.einsum("tf,df->td", grad_pre_all, w_up_low, preferred_element_type=jnp.float32)
        )
        + grad_last
    )
    grad_middle = norm_backward(grad_normed, normal_one, inv_one, norm_gain[0])
    gain_one = jnp.sum(grad_normed * normal_one, 0)
    shift_one = jnp.sum(grad_normed, 0)
    grad_attn_all = gather_rows(grad_middle.astype(jnp.bfloat16))
    grad_out_bias = jnp.sum(grad_attn_all, 0, dtype=jnp.float32)
    grad_w_out = jnp.einsum(
        "th,td->hd", context_all, grad_attn_all, preferred_element_type=jnp.float32
    )
    context_part = jnp.einsum(
        "td,hd->th", grad_attn_all, w_out_low, preferred_element_type=jnp.float32
    )
    grad_context = sum_heads(context_part).astype(jnp.bfloat16).reshape(length, head_count, HD)
    grad_queries, grad_keys, grad_values = attend_back(
        query_rows, key_rows, value_rows, same_seq, score_scale, log_total, grad_context
    )
    grad_qkv = (
        jnp.stack([grad_queries, grad_keys, grad_values], 1)
        .reshape(length, 3, head_count * HD)
        .astype(jnp.bfloat16)
    )
    grad_qkv_all = gather_heads(grad_qkv)
    qkv_totals = jnp.sum(grad_qkv_all, 0, dtype=jnp.float32)
    grad_qv_bias = jnp.stack([qkv_totals[0], qkv_totals[2]])
    grad_w_qkv = jnp.einsum(
        "td,tsh->dsh", tokens_all, grad_qkv_all, preferred_element_type=jnp.float32
    )
    input_part = jnp.einsum(
        "tsh,dsh->td", grad_qkv_all, w_qkv_low, preferred_element_type=jnp.float32
    )
    grad_input = sum_rows(input_part) + grad_middle
    summed = (
        lax.psum(grad_w_qkv.astype(jnp.bfloat16), "dp").astype(jnp.float32),
        lax.psum(grad_qv_bias.astype(jnp.bfloat16), "dp").astype(jnp.float32),
        lax.psum(grad_w_out.astype(jnp.bfloat16), "dp").astype(jnp.float32),
        lax.psum(grad_out_bias.astype(jnp.bfloat16), "dp").astype(jnp.float32),
        lax.psum(grad_w_up.astype(jnp.bfloat16), "dp").astype(jnp.float32),
        lax.psum(grad_up_bias.astype(jnp.bfloat16), "dp").astype(jnp.float32),
        lax.psum(grad_w_down.astype(jnp.bfloat16), "dp").astype(jnp.float32),
        lax.psum(grad_down_bias.astype(jnp.bfloat16), "dp").astype(jnp.float32),
    )
    norm_summed = lax.psum((gain_one, shift_one, gain_two, shift_two), ("dp", "row"))
    grad_norm_gain = jnp.stack([norm_summed[0], norm_summed[2]])
    grad_norm_bias = jnp.stack([norm_summed[1], norm_summed[3]])
    return (
        output,
        grad_input,
        summed[0],
        summed[1],
        summed[2],
        summed[3],
        summed[4],
        summed[5],
        summed[6],
        summed[7],
        grad_norm_gain,
        grad_norm_bias,
    )


def solution(mesh):
    placed = (
        P(("dp", "row"), "col"),
        P(("dp", "col"), None),
        P("col", None, "row"),
        P(None, "row"),
        P("row", "col"),
        P("col"),
        P("col", "row"),
        P("row"),
        P("row", "col"),
        P("col"),
        P(None, "col"),
        P(None, "col"),
        P(("dp", "row"), "col"),
    )
    return jax.shard_map(
        shards,
        mesh=mesh,
        in_specs=placed,
        out_specs=(
            P(("dp", "row"), "col"),
            P(("dp", "row"), "col"),
            P("col", None, "row"),
            P(None, "row"),
            P("row", "col"),
            P("col"),
            P("col", "row"),
            P("row"),
            P("row", "col"),
            P("col"),
            P(None, "col"),
            P(None, "col"),
        ),
        check_vma=False,
    )
```

profile of v0, /device:TPU:1, one launch (start us, length us, event | category | flops | bytes accessed | tf_op | source)
XLA Modules:
  0.0 2170.3 jit_solution(4346176127747635894)
XLA Ops:
  9.5 27.0 %all-gather.9.cloned.1.call-done = bf16[2560,256]{1,0:T(8,128)(2,1)} async-done(((bf16[1280,256]{1,0:T(8,128)(2,1)}), bf16[2560,256]{1,0:T(8,128)(2,1)}) %all-gather.9.cloned.1.call-update) | async-done | bytes 1310736 | tf_op jit(solution)/shard_map/all_gather | solution.py:17
  48.2 260.8 %reduce-scatter.9.cloned.1.call-done = f32[640,3,512]{2,0,1:T(8,128)} async-done(((f32[2560,3,512]{2,0,1:T(8,128)}), f32[640,3,512]{2,0,1:T(8,128)}) %reduce-scatter.9.cloned.1.call-update) | async-done | bytes 3932176 | tf_op jit(solution)/shard_map/reduce_scatter | solution.py:25
  324.3 55.7 %all-gather.11.cloned.1.call-done = bf16[2560,512]{0,1:T(8,128)(2,1)} async-done(((bf16[640,512]{0,1:T(8,128)(2,1)}), bf16[2560,512]{0,1:T(8,128)(2,1)}) %all-gather.11.cloned.1.call-update) | async-done | bytes 2621456 | tf_op jit(solution)/shard_map/all_gather | solution.py:29
  384.3 36.3 %reduce-scatter.11.cloned.1.call-done = f32[1280,256]{1,0:T(8,128)} async-done(((f32[2560,256]{1,0:T(8,128)}), f32[1280,256]{1,0:T(8,128)}) %reduce-scatter.11.cloned.1.call-update) | async-done | bytes 1310736 | tf_op jit(solution)/shard_map/reduce_scatter | solution.py:21
  422.3 15.3 all-reduce.4
  438.9 25.4 %all-gather.13.cloned.1.call-done = bf16[2560,256]{1,0:T(8,128)(2,1)} async-done(((bf16[1280,256]{1,0:T(8,128)(2,1)}), bf16[2560,256]{1,0:T(8,128)(2,1)}) %all-gather.13.cloned.1.call-update) | async-done | bytes 1310736 | tf_op jit(solution)/shard_map/all_gather | solution.py:17
  476.2 347.2 %reduce-scatter.13.cloned.1.call-done = f32[640,2048]{1,0:T(8,128)} async-done(((f32[2560,2048]{1,0:T(8,128)}), f32[640,2048]{1,0:T(8,128)}) %reduce-scatter.13.cloned.1.call-update) | async-done | bytes 5242896 | tf_op jit(solution)/shard_map/reduce_scatter | solution.py:33
  823.4 13.7 multiply_convert_fusion.1
  837.2 185.8 %all-gather.15.cloned.1.call-done = bf16[2560,2048]{1,0:T(8,128)(2,1)} async-done(((bf16[640,2048]{1,0:T(8,128)(2,1)}), bf16[2560,2048]{1,0:T(8,128)(2,1)}) %all-gather.15.cloned.1.call-update) | async-done | bytes 10485776 | tf_op jit(solution)/shard_map/all_gather | solution.py:37
  1032.0 35.6 %reduce-scatter.15.cloned.1.call-done = f32[1280,256]{1,0:T(8,128)} async-done(((f32[2560,256]{1,0:T(8,128)}), f32[1280,256]{1,0:T(8,128)}) %reduce-scatter.15.cloned.1.call-update) | async-done | bytes 1310736 | tf_op jit(solution)/shard_map/reduce_scatter | solution.py:21
  1069.8 15.0 all-reduce.3
  1086.9 12.1 all-reduce.2
  1102.6 28.9 %all-gather.17.cloned.1.call-done = bf16[2560,256]{1,0:T(8,128)(2,1)} async-done(((bf16[1280,256]{1,0:T(8,128)(2,1)}), bf16[2560,256]{1,0:T(8,128)(2,1)}) %all-gather.17.cloned.1.call-update) | async-done | bytes 1310736 | tf_op jit(solution)/shard_map/all_gather | solution.py:17
  1131.6 11.9 fusion.25
  1143.6 347.2 %reduce-scatter.17.cloned.1.call-done = f32[640,2048]{1,0:T(8,128)} async-done(((f32[2560,2048]{1,0:T(8,128)}), f32[640,2048]{1,0:T(8,128)}) %reduce-scatter.17.cloned.1.call-update) | async-done | bytes 5242896 | tf_op jit(solution)/shard_map/reduce_scatter | solution.py:33
  1498.7 185.8 %all-gather.19.cloned.1.call-done = bf16[2560,2048]{1,0:T(8,128)(2,1)} async-done(((bf16[640,2048]{1,0:T(8,128)(2,1)}), bf16[2560,2048]{1,0:T(8,128)(2,1)}) %all-gather.19.cloned.1.call-update) | async-done | bytes 10485776 | tf_op jit(solution)/shard_map/all_gather | solution.py:37
  1693.6 35.6 %reduce-scatter.19.cloned.1.call-done = f32[1280,256]{1,0:T(8,128)} async-done(((f32[2560,256]{1,0:T(8,128)}), f32[1280,256]{1,0:T(8,128)}) %reduce-scatter.19.cloned.1.call-update) | async-done | bytes 1310736 | tf_op jit(solution)/shard_map/reduce_scatter | solution.py:21
  1731.8 15.0 all-reduce.1
  1748.8 25.4 %all-gather.21.cloned.1.call-done = bf16[2560,256]{1,0:T(8,128)(2,1)} async-done(((bf16[1280,256]{1,0:T(8,128)(2,1)}), bf16[2560,256]{1,0:T(8,128)(2,1)}) %all-gather.21.cloned.1.call-update) | async-done | bytes 1310736 | tf_op jit(solution)/shard_map/all_gather | solution.py:17
  1779.3 93.5 %reduce-scatter.21.cloned.1.call-done = f32[640,512]{1,0:T(8,128)} async-done(((f32[2560,512]{1,0:T(8,128)}), f32[640,512]{1,0:T(8,128)}) %reduce-scatter.21.cloned.1.call-update) | async-done | bytes 1310736 | tf_op jit(solution)/shard_map/reduce_scatter | solution.py:25
  1924.2 122.9 %all-gather.23.cloned.1.call-done = bf16[2560,3,512]{2,0,1:T(8,128)(2,1)} async-done(((bf16[640,3,512]{2,0,1:T(8,128)(2,1)}), bf16[2560,3,512]{2,0,1:T(8,128)(2,1)}) %all-gather.23.cloned.1.call-update) | async-done | bytes 7864336 | tf_op jit(solution)/shard_map/all_gather | solution.py:29
  2067.8 14.1 all-reduce
  2096.1 24.9 %all-reduce.9.cloned.1.call-done = (bf16[256,3,512]{0,2,1:T(8,128)(2,1)}, bf16[512,256]{1,0:T(8,128)(2,1)}, bf16[256,2048]{1,0:T(8,128)(2,1)}, bf16[2048,256]{1,0:T(8,128)(2,1)}) async-done(((bf16[256,3,512]{0,2,1:T(8,128)(2,1)}, bf16[512,256]{1,0:T(8,128)(2,1)}, bf16[256,2048]{1,0:T(8,128)(2,1)}, bf16[2048,256]{1,0:T(8,128)(2,1)}), (bf16[256,3,512]{0,2,1:T(8,128)(2,1)}, bf16[512,256]{1,0:T(8,128)(2,1)}, ...) | async-done | bytes 3145744 | tf_op jit(solution)/shard_map/psum | solution.py:206
  2129.7 31.3 %reduce-scatter.23.cloned.1.call-done = f32[1280,256]{1,0:T(8,128)} async-done(((f32[2560,256]{1,0:T(8,128)}), f32[1280,256]{1,0:T(8,128)}) %reduce-scatter.23.cloned.1.call-update) | async-done | bytes 1310736 | tf_op jit(solution)/shard_map/reduce_scatter | solution.py:21
  (156 shorter events, 189.3 us)
Async XLA Ops:
  7.2 29.3 %all-gather.9.cloned.1.call-start = ((), (), s32[]{:S(2)}) async-start(), calls=%async_computation.8 | async-start | bytes 1966080 | tf_op jit(solution)/shard_map/all_gather | solution.py:17
  9.5 299.4 %reduce-scatter.9.cloned.1.call-start = ((), (), s32[]{:S(2)}) async-start(), calls=%async_computation.9 | async-start | bytes 19660800 | tf_op jit(solution)/shard_map/reduce_scatter | solution.py:25
  46.0 333.9 %all-gather.11.cloned.1.call-start = ((), (), s32[]{:S(2)}) async-start(), calls=%async_computation.10 | async-start | bytes 3276800 | tf_op jit(solution)/shard_map/all_gather | solution.py:29
  324.2 60.0 %copy-start.16 = (f32[2,256]{1,0:T(2,128)S(1)}, f32[2,256]{1,0:T(2,128)}, u32[]{:S(2)}) copy-start(f32[2,256]{1,0:T(2,128)} %param.23) | copy-start | bytes 6148
  324.2 60.1 %copy-start.17 = (f32[2,256]{1,0:T(2,128)S(1)}, f32[2,256]{1,0:T(2,128)}, u32[]{:S(2)}) copy-start(f32[2,256]{1,0:T(2,128)} %param.24) | copy-start | bytes 6148
  324.2 96.4 %copy-start.8 = (f32[1280,256]{1,0:T(8,128)S(1)}, f32[1280,256]{1,0:T(8,128)}, u32[]{:S(2)}) copy-start(f32[1280,256]{1,0:T(8,128)} %param.13) | copy-start | bytes 3932164
  324.2 96.4 %copy-start.18 = (f32[256]{0:T(256)S(1)}, f32[256]{0:T(256)}, u32[]{:S(2)}) copy-start(f32[256]{0:T(256)} %param.18) | copy-start | bytes 3076
  324.2 96.3 %reduce-scatter.11.cloned.1.call-start = ((), (), s32[]{:S(2)}) async-start(), calls=%async_computation.11 | async-start | bytes 3932160 | tf_op jit(solution)/shard_map/reduce_scatter | solution.py:21
  384.2 80.1 %all-gather.13.cloned.1.call-start = ((), (), s32[]{:S(2)}) async-start(), calls=%async_computation.12 | async-start | bytes 1966080 | tf_op jit(solution)/shard_map/all_gather | solution.py:17
  438.9 384.5 %reduce-scatter.13.cloned.1.call-start = ((), (), s32[]{:S(2)}) async-start(), calls=%async_computation.13 | async-start | bytes 26214400 | tf_op jit(solution)/shard_map/reduce_scatter | solution.py:33
  476.1 347.2 %copy-start.14 = (f32[2048]{0:T(1024)S(1)}, f32[2048]{0:T(1024)}, u32[]{:S(2)}) copy-start(f32[2048]{0:T(1024)} %param.20) | copy-start | bytes 24580
  476.2 546.8 %all-gather.15.cloned.1.call-start = ((), (), s32[]{:S(2)}) async-start(), calls=%async_computation.14 | async-start | bytes 13107200 | tf_op jit(solution)/shard_map/all_gather | solution.py:37
  837.1 230.6 %copy-start.19 = (f32[256]{0:T(256)S(1)}, f32[256]{0:T(256)}, u32[]{:S(2)}) copy-start(f32[256]{0:T(256)} %param.22) | copy-start | bytes 3076
  837.1 230.6 %reduce-scatter.15.cloned.1.call-start = ((), (), s32[]{:S(2)}) async-start(), calls=%async_computation.15 | async-start | bytes 3932160 | tf_op jit(solution)/shard_map/reduce_scatter | solution.py:21
  1032.0 99.6 %all-gather.17.cloned.1.call-start = ((), (), s32[]{:S(2)}) async-start(), calls=%async_computation.16 | async-start | bytes 1966080 | tf_op jit(solution)/shard_map/all_gather | solution.py:17
  1102.4 388.3 %reduce-scatter.17.cloned.1.call-start = ((), (), s32[]{:S(2)}) async-start(), calls=%async_computation.17 | async-start | bytes 26214400 | tf_op jit(solution)/shard_map/reduce_scatter | solution.py:33
  1143.5 541.0 %all-gather.19.cloned.1.call-start = ((), (), s32[]{:S(2)}) async-start(), calls=%async_computation.18 | async-start | bytes 13107200 | tf_op jit(solution)/shard_map/all_gather | solution.py:37
  1498.7 230.6 %reduce-scatter.19.cloned.1.call-start = ((), (), s32[]{:S(2)}) async-start(), calls=%async_computation.19 | async-start | bytes 3932160 | tf_op jit(solution)/shard_map/reduce_scatter | solution.py:21
  1693.6 80.6 %all-gather.21.cloned.1.call-start = ((), (), s32[]{:S(2)}) async-start(), calls=%async_computation.20 | async-start | bytes 1966080 | tf_op jit(solution)/shard_map/all_gather | solution.py:17
  1748.8 124.0 %reduce-scatter.21.cloned.1.call-start = ((), (), s32[]{:S(2)}) async-start(), calls=%async_computation.21 | async-start | bytes 6553600 | tf_op jit(solution)/shard_map/reduce_scatter | solution.py:25
  1778.8 268.3 %all-gather.23.cloned.1.call-start = ((), (), s32[]{:S(2)}) async-start(), calls=%async_computation.22 | async-start | bytes 9830400 | tf_op jit(solution)/shard_map/all_gather | solution.py:29
  1905.2 215.8 %all-reduce.9.cloned.1.call-start = ((), (), s32[]{:S(2)}) async-start(), calls=%async_computation.24 | async-start | bytes 6291456 | tf_op jit(solution)/shard_map/psum | solution.py:206
  2053.8 107.1 %reduce-scatter.23.cloned.1.call-start = ((), (), s32[]{:S(2)}) async-start(), calls=%async_computation.23 | async-start | bytes 3932160 | tf_op jit(solution)/shard_map/reduce_scatter | solution.py:21
  2087.9 73.1 %copy-start.9 = (f32[1280,256]{1,0:T(8,128)S(1)}, f32[1280,256]{1,0:T(8,128)}, u32[]{:S(2)}) copy-start(f32[1280,256]{1,0:T(8,128)} %get-tuple-element.81) | copy-start | bytes 3932164
  (18 other events, 185.5 us)
Sparse Core Ops, SparseCore 0:
  10.1 26.3 all-gather.8
  46.2 262.6 reduce-scatter.8
  324.3 55.6 all-gather.10
  384.3 36.2 reduce-scatter.10
  439.0 25.2 all-gather.12
  476.3 347.0 reduce-scatter.12
  837.2 185.7 all-gather.14
  1032.1 35.5 reduce-scatter.14
  1102.5 29.0 all-gather.16
  1143.6 347.0 reduce-scatter.16
  1498.8 185.7 all-gather.18
  1693.7 35.5 reduce-scatter.18
  1748.9 25.2 all-gather.20
  1779.0 93.7 reduce-scatter.20
  1905.3 141.7 all-gather.22
  2054.0 66.9 all-reduce.8
  2123.2 37.7 reduce-scatter.22
where the time goes:
time: 2180 us; the launch traced here: 2170 us
  waiting for transfers between devices  1870 us (86%)
  matrix products  121 us (6%)
  other arithmetic  77.2 us (4%)
  blocking collectives  77.2 us (4%)
    reduce_scatter x2, waiting for transfers between devices, sum_hidden(): return lax.psum_scatter(values, 'col', scatter_dimension=0, tiled=True)  694 us
    all_gather x2, waiting for transfers between devices, gather_hidden(): return lax.all_gather(values, 'col', axis=0, tiled=True)  372 us
    reduce_scatter x2, waiting for transfers between devices, sum_heads(): return lax.psum_scatter(values, 'col', scatter_dimension=0, tiled=True)  354 us
    all_gather x2, waiting for transfers between devices, gather_heads(): return lax.all_gather(values, 'col', axis=0, tiled=True)  179 us
    reduce_scatter x4, waiting for transfers between devices, sum_rows(): return lax.psum_scatter(values, 'row', scatter_dimension=0, tiled=True)  139 us
    all_gather x4, waiting for transfers between devices, gather_rows(): return lax.all_gather(values, 'row', axis=0, tiled=True)  107 us
    psum x4, blocking collectives, col_totals(): return lax.psum((first_sum, second_sum), 'col')  57.3 us
  transfers between devices with their start and end apart: 17, of which 17 were waited for; matrix products, arithmetic and copies ran while one was open for 2% of the time, Pallas kernels for 0%

commit v1 on v0

v1 whole, which is shorter than its diff:
```python
from functools import partial
import math

import jax
import jax.numpy as jnp
from jax import lax
from jax.sharding import PartitionSpec as P

HD = 64


EPS = 1e-05


def hop(values, axis, step):
    count = lax.axis_size(axis)
    return lax.ppermute(values, axis, [(i, i ^ step) for i in range(count)])


def bit_of(axis, step):
    return (lax.axis_index(axis) & step) != 0


def in_order(mine, theirs, flag, dim):
    return jnp.stack([jnp.where(flag, theirs, mine), jnp.where(flag, mine, theirs)], dim)


def gather_weight(block):
    dp_count = lax.axis_size("dp")
    col_count = lax.axis_size("col")
    depth = block.shape[0] // dp_count
    piece = lax.dynamic_slice_in_dim(block, lax.axis_index("dp") * depth, depth, 0)
    piece = piece.astype(jnp.bfloat16)
    parts = [piece] + [hop(piece, "col", k) for k in range(1, col_count)]
    step = 1
    while len(parts) > 1:
        flag = bit_of("col", step)
        parts = [in_order(parts[i], parts[i + 1], flag, 0) for i in range(0, len(parts), 2)]
        step *= 2
    held = parts[0].reshape((col_count, 1) + piece.shape)
    step = dp_count // 2
    order = []
    while step:
        order.append(step)
        step //= 2
    for step in order:
        pair = in_order(held, hop(held, "dp", step), bit_of("dp", step), 2)
        held = pair.reshape((col_count, pair.shape[1] * 2) + piece.shape)
    return held.reshape((col_count,) + block.shape)


def reduce_weight(grad):
    dp_count = lax.axis_size("dp")
    col_count = lax.axis_size("col")
    depth = grad.shape[1] // dp_count
    tail = grad.shape[2:]
    held = grad.reshape((col_count, dp_count, depth) + tail)
    step = 1
    while step < dp_count:
        pairs = held.reshape((col_count, held.shape[1] // 2, 2, depth) + tail)
        flag = bit_of("dp", step)
        keep = jnp.where(flag, pairs[:, :, 1], pairs[:, :, 0])
        give = jnp.where(flag, pairs[:, :, 0], pairs[:, :, 1]).astype(jnp.bfloat16)
        got = hop(give, "dp", step)
        held = (keep.astype(jnp.float32) + got.astype(jnp.float32)).astype(jnp.bfloat16)
        step *= 2
    held = held[:, 0]
    here = lax.axis_index("col")
    total = lax.dynamic_index_in_dim(held, here, 0, keepdims=False).astype(jnp.float32)
    for k in range(1, col_count):
        give = lax.dynamic_index_in_dim(held, here ^ k, 0, keepdims=False)
        total = total + hop(give, "col", k).astype(jnp.float32)
    out = total.astype(jnp.bfloat16)[None]
    step = dp_count // 2
    while step:
        pair = in_order(out, hop(out, "dp", step), bit_of("dp", step), 1)
        out = pair.reshape((pair.shape[0] * 2, depth) + tail)
        step //= 2
    return out.reshape((dp_count * depth,) + tail).astype(jnp.float32)


def from_others(values):
    count = lax.axis_size("row")
    return jnp.concatenate(
        [
            lax.ppermute(values, "row", [((i + k) % count, i) for i in range(count)])
            for k in range(1, count)
        ],
        0,
    )


def to_owners(others, mine):
    count = lax.axis_size("row")
    size = mine.shape[0]
    low = others.astype(jnp.bfloat16)
    for k in range(1, count):
        got = lax.ppermute(
            low[(k - 1) * size : k * size], "row", [(i, (i + k) % count) for i in range(count)]
        )
        mine = mine + got.astype(jnp.float32)
    return mine


def owner_perm(rows, cols, k):
    pairs = []
    for r in range(rows):
        for c in range(cols):
            owner = r * cols + (c ^ k)
            pairs.append((r * cols + c, (owner % rows) * cols + owner // rows))
    return pairs


def to_tokens(values):
    rows, cols = lax.axis_size("row"), lax.axis_size("col")
    size = values.shape[0] // cols
    blocks = values.reshape(cols, size, values.shape[1])
    here = lax.axis_index("col")
    own = lax.axis_index("col") * rows + lax.axis_index("row")
    got = []
    for k in range(cols):
        give = lax.dynamic_index_in_dim(blocks, here ^ k, 0, keepdims=False)
        got.append(lax.ppermute(give, ("row", "col"), owner_perm(rows, cols, k)))
    parts, step = got, 1
    while len(parts) > 1:
        flag = ((own % cols) & step) != 0
        parts = [
            jnp.concatenate(
                [
                    jnp.where(flag, parts[i + 1], parts[i]),
                    jnp.where(flag, parts[i], parts[i + 1]),
                ],
                1,
            )
            for i in range(0, len(parts), 2)
        ]
        step *= 2
    return parts[0]


def from_tokens(values):
    rows, cols = lax.axis_size("row"), lax.axis_size("col")
    size, width = values.shape[0], values.shape[1] // cols
    own = lax.axis_index("col") * rows + lax.axis_index("row")
    got = []
    for k in range(cols):
        start = ((own % cols) ^ k) * width
        give = lax.dynamic_slice_in_dim(values, start, width, 1)
        back = [(there, here) for here, there in owner_perm(rows, cols, k)]
        got.append(lax.ppermute(give, ("row", "col"), back))
    parts, step = got, 1
    while len(parts) > 1:
        flag = bit_of("col", step)
        parts = [
            in_order(parts[i], parts[i + 1], flag, 0).reshape((-1, width))
            for i in range(0, len(parts), 2)
        ]
        step *= 2
    return parts[0]


def norm_forward(values, gain_row, shift_row):
    center = jnp.mean(values, -1, keepdims=True)
    spread = jnp.mean(values * values, -1, keepdims=True) - center * center
    inv_std = lax.rsqrt(spread + EPS)
    normal = (values - center) * inv_std
    return (normal * gain_row + shift_row, normal, inv_std)


def norm_backward(grad_out, normal, inv_std, gain_row):
    scaled = grad_out * gain_row
    first = jnp.mean(scaled, -1, keepdims=True)
    second = jnp.mean(scaled * normal, -1, keepdims=True)
    return inv_std * (scaled - first - normal * second)


def dot(first, second):
    return jnp.dot(first, second, preferred_element_type=jnp.float32)


def dot_back(first, second):
    return jnp.einsum("tf,df->td", first, second, preferred_element_type=jnp.float32)


def outer(first, second):
    return jnp.einsum("td,tf->df", first, second, preferred_element_type=jnp.float32)


def masked_scores(query_rows, key_rows, same_seq, score_scale):
    scores = (
        jnp.einsum("qhe,khe->hqk", query_rows, key_rows, preferred_element_type=jnp.float32)
        * score_scale
    )
    return jnp.where(same_seq, scores, -1000000000.0)


def attend(query_rows, key_rows, value_rows, same_seq, score_scale):
    scores = masked_scores(query_rows, key_rows, same_seq, score_scale)
    row_max = jnp.max(scores, -1, keepdims=True)
    exp_scores = jnp.exp(scores - row_max)
    totals = jnp.sum(exp_scores, -1, keepdims=True)
    attn_probs = (exp_scores / totals).astype(jnp.bfloat16)
    context = jnp.einsum("hqk,khe->qhe", attn_probs, value_rows, preferred_element_type=jnp.float32)
    return (context, row_max + jnp.log(totals))


def attend_back(query_rows, key_rows, value_rows, same_seq, score_scale, log_total, grad_context):
    scores = masked_scores(query_rows, key_rows, same_seq, score_scale)
    attn_probs = jnp.exp(scores - log_total)
    grad_probs = jnp.einsum(
        "qhe,khe->hqk", grad_context, value_rows, preferred_element_type=jnp.float32
    )
    grad_values = jnp.einsum(
        "hqk,qhe->khe",
        attn_probs.astype(jnp.bfloat16),
        grad_context,
        preferred_element_type=jnp.float32,
    )
    inner_sum = jnp.sum(attn_probs * grad_probs, -1, keepdims=True)
    grad_scores = (attn_probs * (grad_probs - inner_sum)).astype(jnp.bfloat16)
    grad_queries = (
        jnp.einsum("hqk,khe->qhe", grad_scores, key_rows, preferred_element_type=jnp.float32)
        * score_scale
    )
    grad_keys = (
        jnp.einsum("hqk,qhe->khe", grad_scores, query_rows, preferred_element_type=jnp.float32)
        * score_scale
    )
    return (grad_queries, grad_keys, grad_values)


def shards(
    tokens,
    lengths,
    w_qkv,
    qv_bias,
    w_out,
    out_bias,
    w_up,
    up_bias,
    w_down,
    down_bias,
    norm_gain,
    norm_bias,
    cotangent,
):
    score_scale = 1.0 / math.sqrt(HD)
    gelu_exact = partial(jax.nn.gelu, approximate=False)
    rows, cols = lax.axis_size("row"), lax.axis_size("col")
    here_row, here_col = lax.axis_index("row"), lax.axis_index("col")
    own_tokens = to_tokens(tokens)
    own_low = own_tokens.astype(jnp.bfloat16)
    other_low = from_others(own_low)
    wide = w_qkv.shape[2]
    w_qkv_all = gather_weight(w_qkv.reshape(w_qkv.shape[0], 3 * wide)).reshape(-1, 3 * wide)
    w_out_all = gather_weight(w_out).transpose(1, 0, 2).reshape(w_out.shape[0], -1)
    w_up_all = gather_weight(w_up).reshape(-1, w_up.shape[1])
    w_down_all = gather_weight(w_down).transpose(1, 0, 2).reshape(w_down.shape[0], -1)
    own_cotangent = to_tokens(cotangent)
    small = jnp.concatenate([out_bias, down_bias, norm_gain[0], norm_gain[1], norm_bias[0], norm_bias[1]])
    small = lax.all_gather(small, "col", axis=0).reshape(cols, 6, -1)
    small = small.transpose(1, 0, 2).reshape(6, -1)
    out_bias_all, down_bias_all = small[0], small[1]
    gains, shifts = small[2:4], small[4:6]

    size = own_low.shape[0]
    full_bias = jnp.concatenate([qv_bias[0], jnp.zeros_like(qv_bias[0]), qv_bias[1]])
    qkv = jnp.concatenate(
        [
            (dot(own_low, w_qkv_all) + full_bias).astype(jnp.bfloat16),
            (dot(other_low, w_qkv_all) + full_bias).astype(jnp.bfloat16),
        ],
        0,
    )
    length = qkv.shape[0]
    head_count = wide // HD
    qkv = qkv.reshape(length, 3, head_count, HD)
    query_rows, key_rows, value_rows = qkv[:, 0], qkv[:, 1], qkv[:, 2]
    seq_ends = jnp.cumsum(lengths[0])
    positions = (jnp.arange(length, dtype=jnp.int32) + here_row * size) % length
    segment = jnp.sum((positions[:, None] >= seq_ends[None, :]).astype(jnp.int32), -1)
    same_seq = (segment[:, None] == segment[None, :])[None]
    context, log_total = attend(query_rows, key_rows, value_rows, same_seq, score_scale)
    context = context.reshape(length, wide).astype(jnp.bfloat16)
    attn_other = dot(context[size:], w_out_all)
    attn_out = to_owners(attn_other, dot(context[:size], w_out_all)) + out_bias_all
    normed_one, normal_one, inv_one = norm_forward(own_tokens + attn_out, gains[0], shifts[0])
    normed_own = normed_one.astype(jnp.bfloat16)
    normed_other = from_others(normed_own)
    pre_own = dot(normed_own, w_up_all) + up_bias
    pre_other = dot(normed_other, w_up_all) + up_bias
    hidden_own = gelu_exact(pre_own).astype(jnp.bfloat16)
    hidden_other = gelu_exact(pre_other).astype(jnp.bfloat16)
    mlp_other = dot(hidden_other, w_down_all)
    mlp_out = to_owners(mlp_other, dot(hidden_own, w_down_all)) + down_bias_all
    last, normal_two, inv_two = norm_forward(normed_one + mlp_out, gains[1], shifts[1])
    output = from_tokens(last)
    grad_last = norm_backward(own_cotangent, normal_two, inv_two, gains[1])
    gain_two = jnp.sum(own_cotangent * normal_two, 0)
    shift_two = jnp.sum(own_cotangent, 0)
    mlp_grad_own = grad_last.astype(jnp.bfloat16)
    mlp_grad_other = from_others(mlp_grad_own)
    down_total = jnp.sum(mlp_grad_own, 0, dtype=jnp.float32)
    pre_grad_own = jax.vjp(gelu_exact, pre_own)[1](dot_back(mlp_grad_own, w_down_all))[0]
    pre_grad_own = pre_grad_own.astype(jnp.bfloat16)
    pre_grad_other = jax.vjp(gelu_exact, pre_other)[1](dot_back(mlp_grad_other, w_down_all))[0]
    pre_grad_other = pre_grad_other.astype(jnp.bfloat16)
    normed_part = dot_back(pre_grad_other, w_up_all)
    grad_normed = to_owners(normed_part, dot_back(pre_grad_own, w_up_all)) + grad_last
    pre_grad = jnp.concatenate([pre_grad_own, pre_grad_other], 0)
    up_total = jnp.sum(pre_grad, 0, dtype=jnp.float32)
    down_grad = outer(
        jnp.concatenate([hidden_own, hidden_other], 0),
        jnp.concatenate([mlp_grad_own, mlp_grad_other], 0),
    )
    down_grad = down_grad.astype(jnp.bfloat16).reshape(w_down.shape[0], cols, -1).transpose(1, 0, 2)
    grad_w_down = reduce_weight(down_grad)
    up_grad = outer(jnp.concatenate([normed_own, normed_other], 0), pre_grad).astype(jnp.bfloat16)
    grad_w_up = reduce_weight(up_grad.reshape((cols,) + w_up.shape))
    grad_middle = norm_backward(grad_normed, normal_one, inv_one, gains[0])
    gain_one = jnp.sum(grad_normed * normal_one, 0)
    shift_one = jnp.sum(grad_normed, 0)
    attn_grad_own = grad_middle.astype(jnp.bfloat16)
    attn_grad_other = from_others(attn_grad_own)
    out_total = jnp.sum(attn_grad_own, 0, dtype=jnp.float32)
    grad_context = jnp.concatenate(
        [
            dot_back(attn_grad_own, w_out_all).astype(jnp.bfloat16),
            dot_back(attn_grad_other, w_out_all).astype(jnp.bfloat16),
        ],
        0,
    ).reshape(length, head_count, HD)
    out_grad = outer(context, jnp.concatenate([attn_grad_own, attn_grad_other], 0))
    out_grad = out_grad.astype(jnp.bfloat16).reshape(w_out.shape[0], cols, -1).transpose(1, 0, 2)
    grad_w_out = reduce_weight(out_grad)
    grad_queries, grad_keys, grad_values = attend_back(
        query_rows, key_rows, value_rows, same_seq, score_scale, log_total, grad_context
    )
    grad_qkv = (
        jnp.stack([grad_queries, grad_keys, grad_values], 1)
        .reshape(length, 3 * wide)
        .astype(jnp.bfloat16)
    )
    qkv_totals = jnp.sum(grad_qkv, 0, dtype=jnp.float32)
    qkv_grad = outer(jnp.concatenate([own_low, other_low], 0), grad_qkv).astype(jnp.bfloat16)
    grad_w_qkv = reduce_weight(qkv_grad.reshape(cols, -1, 3 * wide)).reshape(w_qkv.shape)
    input_other = dot_back(grad_qkv[size:], w_qkv_all)
    grad_own = to_owners(input_other, dot_back(grad_qkv[:size], w_qkv_all)) + grad_middle
    grad_input = from_tokens(grad_own)

    everywhere = lax.psum(
        jnp.stack([out_total, down_total, gain_one, gain_two, shift_one, shift_two]),
        ("dp", "row", "col"),
    )
    part = everywhere.shape[1] // cols
    mine = lax.dynamic_slice_in_dim(everywhere, here_col * part, part, 1)
    halves = lax.psum(
        jnp.concatenate([up_total, qkv_totals[:wide], qkv_totals[2 * wide :]]), ("dp", "col")
    )
    hid = up_total.shape[0]
    return (
        output,
        grad_input,
        grad_w_qkv,
        halves[hid:].reshape(2, wide),
        grad_w_out,
        mine[0],
        grad_w_up,
        halves[:hid],
        grad_w_down,
        mine[1],
        mine[2:4],
        mine[4:6],
    )


def solution(mesh):
    placed = (
        P(("dp", "row"), "col"),
        P(("dp", "col"), None),
        P("col", None, "row"),
        P(None, "row"),
        P("row", "col"),
        P("col"),
        P("col", "row"),
        P("row"),
        P("row", "col"),
        P("col"),
        P(None, "col"),
        P(None, "col"),
        P(("dp", "row"), "col"),
    )
    return jax.shard_map(
        shards,
        mesh=mesh,
        in_specs=placed,
        out_specs=(
            P(("dp", "row"), "col"),
            P(("dp", "row"), "col"),
            P("col", None, "row"),
            P(None, "row"),
            P("row", "col"),
            P("col"),
            P("col", "row"),
            P("row"),
            P("row", "col"),
            P("col"),
            P(None, "col"),
            P(None, "col"),
        ),
        check_vma=False,
    )
```

time: 2180 us -> 778 us (0.36)
  waiting for transfers between devices: 1870 us -> 192 us
  starting transfers between devices: 1.71 us -> 208 us
  local copies, waits for them, and re-layouts: 9.35 us -> 81.2 us
  blocking collectives: 77.2 us -> 119 us
  matrix products: 121 us -> 87.3 us
    reduce_scatter x8 -> x0, waiting for transfers between devices: 1190 us -> none  [the longest x2 694 us: sum_hidden(): return lax.psum_scatter(values, 'col', scatter_dimension=0, tiled=True)]
    all_gather x8 -> x0, waiting for transfers between devices: 657 us -> none  [the longest x2 372 us: gather_hidden(): return lax.all_gather(values, 'col', axis=0, tiled=True)]
    ppermute x0 -> x72, starting transfers between devices: none -> 208 us  [the longest x48 116 us: hop(): return lax.ppermute(values, axis, [(i, i ^ step) for i in range(count)])]
    ppermute x0 -> x72, waiting for transfers between devices: none -> 192 us  [the longest x48 99.4 us: hop(): return lax.ppermute(values, axis, [(i, i ^ step) for i in range(count)])]
    convert_element_type x15 -> x10, other arithmetic: 42.9 us -> 7.28 us  [the longest x4 3.78 us: reduce_weight(): return out.reshape((dp_count * depth,) + tail).astype(jnp.float32)]
    dot_general x12 -> x20, matrix products: 93.1 us -> 62.5 us  [the longest x8 25.7 us: dot(): return jnp.dot(first, second, preferred_element_type=jnp.float32)]
    psum x6 -> x2, blocking collectives: 77.2 us -> 107 us  [the longest x1 58.3 us: shards(): lax.psum(jnp.concatenate([up_total, qkv_totals[:wide], qkv_totals[2 * wid...]
    unnamed x51 -> x126, local copies, waits for them, and re-layouts: 6.11 us -> 32 us
  transfers between devices with their start and end apart: 17 -> 72, of which waited for: 17 -> 17; matrix products, arithmetic and copies ran while one was open for 2% -> 25% of each run, Pallas kernels for 0% -> 0%
where the time goes in v1:
time: 778 us; the launch traced here: 766 us
  starting transfers between devices  208 us (27%)
  waiting for transfers between devices  192 us (25%)
  blocking collectives  119 us (15%)
  matrix products  87.3 us (11%)
  local copies, waits for them, and re-layouts  81.2 us (10%)
  other arithmetic  75.6 us (10%)
    ppermute x48, starting transfers between devices, hop(): return lax.ppermute(values, axis, [(i, i ^ step) for i in range(count)])  116 us
    ppermute x48, waiting for transfers between devices, hop(): return lax.ppermute(values, axis, [(i, i ^ step) for i in range(count)])  99.4 us
    psum x1, blocking collectives, shards(): lax.psum(jnp.concatenate([up_total, qkv_totals[:wide], qkv_totals[2 * wid...  58.3 us
    psum x1, blocking collectives, shards(): lax.psum(jnp.stack([out_total, down_total, gain_one, gain_two, shift_one,...  48.7 us
    ppermute x8, starting transfers between devices, from_tokens(): got.append(lax.ppermute(give, ('row', 'col'), back))  41.1 us
    ppermute x8, starting transfers between devices, to_tokens(): got.append(lax.ppermute(give, ('row', 'col'), owner_perm(rows, cols, k)))  34 us
    unnamed x126, local copies, waits for them, and re-layouts  32 us
    ppermute x8, waiting for transfers between devices, to_tokens(): got.append(lax.ppermute(give, ('row', 'col'), owner_perm(rows, cols, k)))  30.7 us
  transfers between devices with their start and end apart: 72, of which 17 were waited for; matrix products, arithmetic and copies ran while one was open for 25% of the time, Pallas kernels for 0%

profile of v1, /device:TPU:1, one launch (start us, length us, event | category | flops | bytes accessed | tf_op | source)
XLA Modules:
  0.0 765.7 jit_solution(14080815982191101653)
XLA Ops:
  16.0 12.2 %all-gather.1 = f32[4,1,1536]{2,1,0:T(1,128)S(1)} all-gather(f32[1,1,1536]{2,1,0:T(1,128)S(1)} %reshape.1143), channel_id=2, replica_groups=mesh['dp'=4,'row'=2,'col'=4] {'col'}, dimensions={0}, use_global_device_ids=true | all-gather | bytes 30720 | tf_op jit(solution)/shard_map/all_gather | solution.py:261
  42.4 16.7 %collective-permute-done.6 = bf16[64,1536]{0,1:T(8,128)(2,1)S(1)} collective-permute-done((bf16[64,1536]{0,1:T(8,128)(2,1)S(1)}, bf16[64,1536]{0,1:T(8,128)(2,1)S(1)}, u32[]{:S(2)}, u32[]{:S(2)}) %collective-permute-start.6) | collective-permute-done | bytes 196640 | tf_op jit(solution)/shard_map/ppermute | solution.py:17
  59.4 13.1 %collective-permute-start.18 = (bf16[64,2048]{1,0:T(8,128)(2,1)S(1)}, bf16[64,2048]{1,0:T(8,128)(2,1)S(1)}, u32[]{:S(2)}, u32[]{:S(2)}) collective-permute-start(bf16[64,2048]{1,0:T(8,128)(2,1)S(1)} %copy-done.48), channel_id=1, source_target_pairs={{0,1},{1,0},{2,3},{3,2},{4,5},{5,4},{6,7},{7,6},{8,9},{9,8},{10,11... | collective-permute-start | bytes 786440 | tf_op jit(solution)/shard_map/ppermute | solution.py:17
  72.5 10.3 %collective-permute-start.17 = (bf16[64,2048]{1,0:T(8,128)(2,1)S(1)}, bf16[64,2048]{1,0:T(8,128)(2,1)S(1)}, u32[]{:S(2)}, u32[]{:S(2)}) collective-permute-start(bf16[64,2048]{1,0:T(8,128)(2,1)S(1)} %copy-done.48), channel_id=1, source_target_pairs={{0,2},{1,3},{2,0},{3,1},{4,6},{5,7},{6,4},{7,5},{8,10},{9,11},{10,... | collective-permute-start | bytes 786440 | tf_op jit(solution)/shard_map/ppermute | solution.py:17
  96.4 32.4 %collective-permute-done.17 = bf16[64,2048]{1,0:T(8,128)(2,1)S(1)} collective-permute-done((bf16[64,2048]{1,0:T(8,128)(2,1)S(1)}, bf16[64,2048]{1,0:T(8,128)(2,1)S(1)}, u32[]{:S(2)}, u32[]{:S(2)}) %collective-permute-start.17) | collective-permute-done | bytes 262176 | tf_op jit(solution)/shard_map/ppermute | solution.py:17
  145.9 30.7 %collective-permute-done.1 = f32[320,256]{1,0:T(8,128)S(1)} collective-permute-done((f32[320,256]{1,0:T(8,128)S(1)}, f32[320,256]{1,0:T(8,128)S(1)}, u32[]{:S(2)}, u32[]{:S(2)}) %collective-permute-start.1) | collective-permute-done | bytes 327712 | tf_op jit(solution)/shard_map/ppermute | solution.py:123
  185.6 17.0 %collective-permute-done.24 = bf16[4,1,512,256]{3,2,0,1:T(8,128)(2,1)} collective-permute-done((bf16[4,1,512,256]{3,2,0,1:T(8,128)(2,1)}, bf16[4,1,512,256]{3,2,0,1:T(8,128)(2,1)}, u32[]{:S(2)}, u32[]{:S(2)}) %collective-permute-start.24) | collective-permute-done | bytes 1048608 | tf_op jit(solution)/shard_map/ppermute | solution.py:17
  202.6 18.3 %collective-permute-start.34 = (f32[320,256]{1,0:T(8,128)S(1)}, f32[320,256]{1,0:T(8,128)}, u32[]{:S(2)}, u32[]{:S(2)}) collective-permute-start(f32[320,256]{1,0:T(8,128)S(1)} %copy-done.46), channel_id=1, source_target_pairs={{0,4},{1,0},{2,5},{3,1},{4,6},{5,2},{6,7},{7,3},{8,12},{9,8},{10,1... | collective-permute-start | bytes 983048 | tf_op jit(solution)/shard_map/ppermute | solution.py:123
  235.0 16.0 %collective-permute-done.9 = bf16[320,1024]{1,0:T(8,128)(2,1)S(1)} collective-permute-done((bf16[320,1024]{1,0:T(8,128)(2,1)S(1)}, bf16[320,1024]{1,0:T(8,128)(2,1)S(1)}, u32[]{:S(2)}, u32[]{:S(2)}) %collective-permute-start.9) | collective-permute-done | bytes 655392 | tf_op jit(solution)/shard_map/ppermute | solution.py:86
  273.8 11.2 %collective-permute-done.15 = bf16[320,1024]{1,0:T(8,128)(2,1)S(1)} collective-permute-done((bf16[320,1024]{1,0:T(8,128)(2,1)S(1)}, bf16[320,1024]{1,0:T(8,128)(2,1)S(1)}, u32[]{:S(2)}, u32[]{:S(2)}) %collective-permute-start.15) | collective-permute-done | bytes 655392 | tf_op jit(solution)/shard_map/ppermute | solution.py:98
  302.7 10.3 %multiply_convert_fusion.1 = (bf16[320,2048]{1,0:T(8,128)(2,1)S(1)}, f32[320,2048]{1,0:T(8,128)}, f32[320,2048]{1,0:T(8,128)}) fusion(f32[2048]{0:T(1024)S(1)} %copy-done.53, bf16[320,1024]{1,0:T(8,128)(2,1)} %collective-permute-done.26, bf16[1024,2048]{1,0:T(8,128)(2,1)S(1)} %bitcast.499), kind=kOutput, calls=%fused_computation.43 | convolution fusion | flops 1385431040 | bytes 11411456 | tf_op jit(solution)/shard_map/dot_general | solution.py:178
  315.3 8.0 %multiply_convert_fusion.2 = (bf16[320,2048]{1,0:T(8,128)(2,1)S(1)}, f32[320,2048]{1,0:T(8,128)S(1)}, f32[320,2048]{1,0:T(8,128)S(1)}) fusion(f32[2048]{0:T(1024)S(1)} %copy-done.53, bf16[320,1024]{1,0:T(8,128)(2,1)} %fusion.52, bf16[1024,2048]{1,0:T(8,128)(2,1)S(1)} %bitcast.500), kind=kOutput, calls=%fused_computation.56 | convolution fusion | flops 1385431040 | bytes 11411456 | tf_op jit(solution)/shard_map/dot_general | solution.py:178
  337.3 14.7 %collective-permute-start.30 = (f32[320,256]{1,0:T(8,128)S(1)}, f32[320,256]{1,0:T(8,128)S(1)}, u32[]{:S(2)}, u32[]{:S(2)}) collective-permute-start(f32[320,256]{1,0:T(8,128)S(1)} %get-tuple-element.112), channel_id=1, source_target_pairs={{4,0},{0,1},{5,2},{1,3},{6,4},{2,5},{7,6},{3,7},{12,8},{8,9},{13,1... | collective-permute-start | bytes 983048 | tf_op jit(solution)/shard_map/ppermute | solution.py:150
  416.7 8.9 %copy.196 = bf16[4,2,1,512,256]{4,3,0,1,2:T(8,128)(2,1)S(1)} copy(bf16[4,2,1,512,256]{3,2,1,4,0:T(2,128)(2,1)} %get-tuple-element.75) | data formatting | bytes 4194304
  425.6 10.5 %copy.197 = bf16[4,2,1,512,256]{4,3,0,1,2:T(8,128)(2,1)} copy(bf16[4,2,1,512,256]{3,2,1,4,0:T(2,128)(2,1)} %get-tuple-element.76) | data formatting | bytes 4194304
  444.7 48.7 %psum.15 = f32[6,1024]{1,0:T(8,128)S(1)} all-reduce(f32[6,1024]{1,0:T(8,128)S(1)} %stack.403), channel_id=1, replica_groups=mesh['dp'=4,'row'=2,'col'=4] {'dp','row','col'}, use_global_device_ids=true, to_apply=%region_22.23 | all-reduce | flops 6144 | bytes 49152 | tf_op jit(solution)/shard_map/psum | solution.py:351
  505.4 9.4 %multiply_reduce_fusion = (f32[8,640]{1,0:T(8,128)S(1)}, f32[8,640,640]{1,2,0:T(8,128)}) fusion(f32[8,640,640]{1,2,0:T(8,128)} %copy-done, f32[8,640]{1,0:T(8,128)S(1)} %log_add_fusion, bf16[640,8,64]{0,2,1:T(8,128)(2,1)S(1)} %bitcast.493, bf16[640,3,8,64]{0,3,2,1:T(8,128)(2,1)S(1)} %bitcast.487), kind=kOutput, calls=%fused_computation.1 | convolution fusion | flops 429255680 | bytes 27566080 | tf_op jit(solution)/shard_map/qhe,khe->hqk/dot_general | solution.py:210
  526.3 58.3 %psum.14 = f32[3072]{0:T(1024)S(1)} all-reduce(f32[3072]{0:T(1024)S(1)} %pad_maximum_fusion.34), channel_id=1, replica_groups=mesh['dp'=4,'row'=2,'col'=4] {'dp','col'}, use_global_device_ids=true, to_apply=%region_15.16 | all-reduce | flops 3072 | bytes 24576 | tf_op jit(solution)/shard_map/psum | solution.py:357
  610.2 11.7 %collective-permute-done.39 = bf16[320,1024]{1,0:T(8,128)(2,1)S(1)} collective-permute-done((bf16[320,1024]{1,0:T(8,128)(2,1)S(1)}, bf16[320,1024]{1,0:T(8,128)(2,1)S(1)}, u32[]{:S(2)}, u32[]{:S(2)}) %collective-permute-start.39) | collective-permute-done | bytes 655392 | tf_op jit(solution)/shard_map/ppermute | solution.py:98
  635.0 8.5 %collective-permute-start.42 = (f32[320,256]{1,0:T(8,128)S(1)}, f32[320,256]{1,0:T(8,128)S(1)}, u32[]{:S(2)}, u32[]{:S(2)}) collective-permute-start(f32[320,256]{1,0:T(8,128)S(1)} %get-tuple-element.100), channel_id=1, source_target_pairs={{4,0},{0,1},{5,2},{1,3},{6,4},{2,5},{7,6},{3,7},{12,8},{8,9},{13,1... | collective-permute-start | bytes 983048 | tf_op jit(solution)/shard_map/ppermute | solution.py:150
  658.5 12.2 %collective-permute-done.41 = f32[320,256]{1,0:T(8,128)S(1)} collective-permute-done((f32[320,256]{1,0:T(8,128)S(1)}, f32[320,256]{1,0:T(8,128)S(1)}, u32[]{:S(2)}, u32[]{:S(2)}) %collective-permute-start.41) | collective-permute-done | bytes 327712 | tf_op jit(solution)/shard_map/ppermute | solution.py:150
  683.2 14.0 %collective-permute-done.66 = bf16[4,1,512,256]{3,2,1,0:T(8,128)(2,1)S(1)} collective-permute-done((bf16[4,1,512,256]{3,2,1,0:T(8,128)(2,1)S(1)}, bf16[4,1,512,256]{3,2,1,0:T(8,128)(2,1)S(1)}, u32[]{:S(2)}, u32[]{:S(2)}) %collective-permute-start.66) | collective-permute-done | bytes 1048608 | tf_op jit(solution)/shard_map/ppermute | solution.py:17
  728.0 12.5 %collective-permute-start.64 = (bf16[2,64,2048]{2,1,0:T(8,128)(2,1)S(1)}, bf16[2,64,2048]{2,1,0:T(8,128)(2,1)S(1)}, u32[]{:S(2)}, u32[]{:S(2)}) collective-permute-start(bf16[2,64,2048]{2,1,0:T(8,128)(2,1)S(1)} %maximum_bitcast_fusion.4), channel_id=1, source_target_pairs={{0,8},{8,0},{16,24},{24,16},{1,9},{9,1},{17,25},{25,17},{2,10},{10... | collective-permute-start | bytes 1572872 | tf_op jit(solution)/shard_map/ppermute | solution.py:17
  742.5 10.2 %collective-permute-start.71 = (bf16[2,512,256]{2,1,0:T(8,128)(2,1)S(1)}, bf16[2,512,256]{2,1,0:T(8,128)(2,1)S(1)}, u32[]{:S(2)}, u32[]{:S(2)}) collective-permute-start(bf16[2,512,256]{2,1,0:T(8,128)(2,1)S(1)} %maximum_bitcast_fusion.5), channel_id=1, source_target_pairs={{0,8},{8,0},{16,24},{24,16},{1,9},{9,1},{17,25},{25,17},{2,10},{10... | collective-permute-start | bytes 1572872 | tf_op jit(solution)/shard_map/ppermute | solution.py:17
  (430 shorter events, 347.6 us)
Async XLA Ops:
  7.9 83.4 %collective-permute-start.23 = (bf16[512,256]{1,0:T(8,128)(2,1)}, bf16[512,256]{1,0:T(8,128)(2,1)}, u32[]{:S(2)}, u32[]{:S(2)}) collective-permute-start(bf16[512,256]{1,0:T(8,128)(2,1)} %dynamic-slice_convert_fusion.1), channel_id=1, source_target_pairs={{0,1},{1,0},{2,3},{3,2},{4,5},{5,4},{6,7},{7,6},{8,9},{9,8},{10,11... | collective-permute-start | bytes 786440 | tf_op jit(solution)/shard_map/ppermute | solution.py:17
  8.3 77.5 %collective-permute-start.22 = (bf16[512,256]{1,0:T(8,128)(2,1)}, bf16[512,256]{1,0:T(8,128)(2,1)}, u32[]{:S(2)}, u32[]{:S(2)}) collective-permute-start(bf16[512,256]{1,0:T(8,128)(2,1)} %dynamic-slice_convert_fusion.1), channel_id=1, source_target_pairs={{0,2},{1,3},{2,0},{3,1},{4,6},{5,7},{6,4},{7,5},{8,10},{9,11},{10,... | collective-permute-start | bytes 786440 | tf_op jit(solution)/shard_map/ppermute | solution.py:17
  36.1 52.6 %collective-permute-start.21 = (bf16[512,256]{1,0:T(8,128)(2,1)}, bf16[512,256]{1,0:T(8,128)(2,1)S(1)}, u32[]{:S(2)}, u32[]{:S(2)}) collective-permute-start(bf16[512,256]{1,0:T(8,128)(2,1)} %dynamic-slice_convert_fusion.1), channel_id=1, source_target_pairs={{0,3},{1,2},{2,1},{3,0},{4,7},{5,6},{6,5},{7,4},{8,11},{9,10},{10,... | collective-permute-start | bytes 786440 | tf_op jit(solution)/shard_map/ppermute | solution.py:17
  72.5 56.3 %collective-permute-start.17 = (bf16[64,2048]{1,0:T(8,128)(2,1)S(1)}, bf16[64,2048]{1,0:T(8,128)(2,1)S(1)}, u32[]{:S(2)}, u32[]{:S(2)}) collective-permute-start(bf16[64,2048]{1,0:T(8,128)(2,1)S(1)} %copy-done.48), channel_id=1, source_target_pairs={{0,2},{1,3},{2,0},{3,1},{4,6},{5,7},{6,4},{7,5},{8,10},{9,11},{10,... | collective-permute-start | bytes 786440 | tf_op jit(solution)/shard_map/ppermute | solution.py:17
  84.4 44.4 %collective-permute-start.16 = (bf16[64,2048]{1,0:T(8,128)(2,1)S(1)}, bf16[64,2048]{1,0:T(8,128)(2,1)S(1)}, u32[]{:S(2)}, u32[]{:S(2)}) collective-permute-start(bf16[64,2048]{1,0:T(8,128)(2,1)S(1)} %copy-done.48), channel_id=1, source_target_pairs={{0,3},{1,2},{2,1},{3,0},{4,7},{5,6},{6,5},{7,4},{8,11},{9,10},{10,... | collective-permute-start | bytes 786440 | tf_op jit(solution)/shard_map/ppermute | solution.py:17
  85.8 59.9 %collective-permute-start = (f32[320,256]{1,0:T(8,128)}, f32[320,256]{1,0:T(8,128)S(1)}, u32[]{:S(2)}, u32[]{:S(2)}) collective-permute-start(f32[320,256]{1,0:T(8,128)} %get-tuple-element.116), channel_id=1, source_target_pairs={{0,5},{1,1},{2,4},{3,0},{4,7},{5,3},{6,6},{7,2},{8,13},{9,9},{10,1... | collective-permute-start | bytes 983048 | tf_op jit(solution)/shard_map/ppermute | solution.py:123
  88.7 51.7 %collective-permute-start.3 = (f32[320,256]{1,0:T(8,128)}, f32[320,256]{1,0:T(8,128)S(1)}, u32[]{:S(2)}, u32[]{:S(2)}) collective-permute-start(f32[320,256]{1,0:T(8,128)} %get-tuple-element.117), channel_id=1, source_target_pairs={{0,0},{1,4},{2,1},{3,5},{4,2},{5,6},{6,3},{7,7},{8,8},{9,12},{10,9... | collective-permute-start | bytes 983048 | tf_op jit(solution)/shard_map/ppermute | solution.py:123
  91.4 52.9 %collective-permute-start.2 = (f32[320,256]{1,0:T(8,128)}, f32[320,256]{1,0:T(8,128)S(1)}, u32[]{:S(2)}, u32[]{:S(2)}) collective-permute-start(f32[320,256]{1,0:T(8,128)} %get-tuple-element.118), channel_id=1, source_target_pairs={{0,4},{1,0},{2,5},{3,1},{4,6},{5,2},{6,7},{7,3},{8,12},{9,8},{10,1... | collective-permute-start | bytes 983048 | tf_op jit(solution)/shard_map/ppermute | solution.py:123
  128.8 47.7 %collective-permute-start.1 = (f32[320,256]{1,0:T(8,128)S(1)}, f32[320,256]{1,0:T(8,128)S(1)}, u32[]{:S(2)}, u32[]{:S(2)}) collective-permute-start(f32[320,256]{1,0:T(8,128)S(1)} %copy-done.47), channel_id=1, source_target_pairs={{0,1},{1,5},{2,0},{3,4},{4,3},{5,7},{6,2},{7,6},{8,9},{9,13},{10,8... | collective-permute-start | bytes 983048 | tf_op jit(solution)/shard_map/ppermute | solution.py:123
  136.0 135.3 %collective-permute-start.32 = (f32[320,256]{1,0:T(8,128)}, f32[320,256]{1,0:T(8,128)}, u32[]{:S(2)}, u32[]{:S(2)}) collective-permute-start(f32[320,256]{1,0:T(8,128)} %get-tuple-element.104), channel_id=1, source_target_pairs={{0,5},{1,1},{2,4},{3,0},{4,7},{5,3},{6,6},{7,2},{8,13},{9,9},{10,1... | collective-permute-start | bytes 983048 | tf_op jit(solution)/shard_map/ppermute | solution.py:123
  140.5 127.4 %collective-permute-start.35 = (f32[320,256]{1,0:T(8,128)}, f32[320,256]{1,0:T(8,128)}, u32[]{:S(2)}, u32[]{:S(2)}) collective-permute-start(f32[320,256]{1,0:T(8,128)} %get-tuple-element.105), channel_id=1, source_target_pairs={{0,0},{1,4},{2,1},{3,5},{4,2},{5,6},{6,3},{7,7},{8,8},{9,12},{10,9... | collective-permute-start | bytes 983048 | tf_op jit(solution)/shard_map/ppermute | solution.py:123
  144.3 34.7 %collective-permute-start.7 = (bf16[4,1,64,1536]{3,2,0,1:T(8,128)(2,1)S(1)}, bf16[4,1,64,1536]{3,2,0,1:T(8,128)(2,1)S(1)}, u32[]{:S(2)}, u32[]{:S(2)}) collective-permute-start(bf16[4,1,64,1536]{3,2,0,1:T(8,128)(2,1)S(1)} %copy.145), channel_id=1, source_target_pairs={{0,16},{8,24},{16,0},{24,8},{1,17},{9,25},{17,1},{25,9},{2,18},{10... | collective-permute-start | bytes 2359304 | tf_op jit(solution)/shard_map/ppermute | solution.py:17
  145.6 78.5 %collective-permute-start.19 = (bf16[4,1,64,2048]{3,2,0,1:T(8,128)(2,1)S(1)}, bf16[4,1,64,2048]{3,2,0,1:T(8,128)(2,1)}, u32[]{:S(2)}, u32[]{:S(2)}) collective-permute-start(bf16[4,1,64,2048]{3,2,0,1:T(8,128)(2,1)S(1)} %bitcast.494), channel_id=1, source_target_pairs={{0,16},{8,24},{16,0},{24,8},{1,17},{9,25},{17,1},{25,9},{2,18},{10... | collective-permute-start | bytes 3145736 | tf_op jit(solution)/shard_map/ppermute | solution.py:17
  181.8 46.8 %collective-permute-start.8 = (bf16[4,2,64,1536]{3,2,1,0:T(8,128)(2,1)}, bf16[4,2,64,1536]{3,2,1,0:T(8,128)(2,1)}, u32[]{:S(2)}, u32[]{:S(2)}) collective-permute-start(bf16[4,2,64,1536]{3,2,1,0:T(8,128)(2,1)} %maximum_bitcast_fusion.2), channel_id=1, source_target_pairs={{0,8},{8,0},{16,24},{24,16},{1,9},{9,1},{17,25},{25,17},{2,10},{10... | collective-permute-start | bytes 4718600 | tf_op jit(solution)/shard_map/ppermute | solution.py:17
  202.6 65.3 %collective-permute-start.34 = (f32[320,256]{1,0:T(8,128)S(1)}, f32[320,256]{1,0:T(8,128)}, u32[]{:S(2)}, u32[]{:S(2)}) collective-permute-start(f32[320,256]{1,0:T(8,128)S(1)} %copy-done.46), channel_id=1, source_target_pairs={{0,4},{1,0},{2,5},{3,1},{4,6},{5,2},{6,7},{7,3},{8,12},{9,8},{10,1... | collective-permute-start | bytes 983048 | tf_op jit(solution)/shard_map/ppermute | solution.py:123
  224.7 46.7 %collective-permute-start.33 = (f32[320,256]{1,0:T(8,128)S(1)}, f32[320,256]{1,0:T(8,128)}, u32[]{:S(2)}, u32[]{:S(2)}) collective-permute-start(f32[320,256]{1,0:T(8,128)S(1)} %copy-done.45), channel_id=1, source_target_pairs={{0,1},{1,5},{2,0},{3,4},{4,3},{5,7},{6,2},{7,6},{8,9},{9,13},{10,8... | collective-permute-start | bytes 983048 | tf_op jit(solution)/shard_map/ppermute | solution.py:123
  251.0 37.1 %collective-permute-start.25 = (bf16[4,2,512,256]{3,2,1,0:T(8,128)(2,1)}, bf16[4,2,512,256]{3,2,1,0:T(8,128)(2,1)}, u32[]{:S(2)}, u32[]{:S(2)}) collective-permute-start(bf16[4,2,512,256]{3,2,1,0:T(8,128)(2,1)} %maximum_bitcast_fusion.1), channel_id=1, source_target_pairs={{0,8},{8,0},{16,24},{24,16},{1,9},{9,1},{17,25},{25,17},{2,10},{10... | collective-permute-start | bytes 6291464 | tf_op jit(solution)/shard_map/ppermute | solution.py:17
  389.4 46.7 %collective-permute-start.37 = (bf16[320,1024]{1,0:T(8,128)(2,1)}, bf16[320,1024]{1,0:T(8,128)(2,1)}, u32[]{:S(2)}, u32[]{:S(2)}) collective-permute-start(bf16[320,1024]{1,0:T(8,128)(2,1)} %convolution_convert_fusion.5), channel_id=1, source_target_pairs={{0,4},{4,0},{1,5},{5,1},{2,6},{6,2},{3,7},{7,3},{8,12},{12,8},{9,1... | collective-permute-start | bytes 1966088 | tf_op jit(solution)/shard_map/ppermute | solution.py:98
  404.6 220.0 %collective-permute-start.58 = (bf16[4,2,64,2048]{3,2,1,0:T(8,128)(2,1)}, bf16[4,2,64,2048]{3,2,1,0:T(8,128)(2,1)}, u32[]{:S(2)}, u32[]{:S(2)}) collective-permute-start(bf16[4,2,64,2048]{3,2,1,0:T(8,128)(2,1)} %fusion.26), channel_id=1, source_target_pairs={{0,8},{8,0},{16,24},{24,16},{1,9},{9,1},{17,25},{25,17},{2,10},{10... | collective-permute-start | bytes 6291464 | tf_op jit(solution)/shard_map/ppermute | solution.py:17
  440.5 55.8 %collective-permute-start.38 = (bf16[320,1024]{1,0:T(8,128)(2,1)}, bf16[320,1024]{1,0:T(8,128)(2,1)}, u32[]{:S(2)}, u32[]{:S(2)}) collective-permute-start(bf16[320,1024]{1,0:T(8,128)(2,1)} %get-tuple-element.64), channel_id=1, source_target_pairs={{4,0},{0,4},{5,1},{1,5},{6,2},{2,6},{7,3},{3,7},{12,8},{8,12},{13,... | collective-permute-start | bytes 1966088 | tf_op jit(solution)/shard_map/ppermute | solution.py:86
  442.6 186.3 %collective-permute-start.65 = (bf16[4,2,512,256]{3,2,0,1:T(8,128)(2,1)}, bf16[4,2,512,256]{3,2,0,1:T(8,128)(2,1)}, u32[]{:S(2)}, u32[]{:S(2)}) collective-permute-start(bf16[4,2,512,256]{3,2,0,1:T(8,128)(2,1)} %select_bitcast_fusion), channel_id=1, source_target_pairs={{0,8},{8,0},{16,24},{24,16},{1,9},{9,1},{17,25},{25,17},{2,10},{10... | collective-permute-start | bytes 6291464 | tf_op jit(solution)/shard_map/ppermute | solution.py:17
  600.9 72.5 %collective-permute-start.44 = (bf16[4,2,64,1536]{3,2,0,1:T(8,128)(2,1)S(1)}, bf16[4,2,64,1536]{3,2,0,1:T(8,128)(2,1)S(1)}, u32[]{:S(2)}, u32[]{:S(2)}) collective-permute-start(bf16[4,2,64,1536]{3,2,0,1:T(8,128)(2,1)S(1)} %select_bitcast_fusion.5), channel_id=1, source_target_pairs={{0,8},{8,0},{16,24},{24,16},{1,9},{9,1},{17,25},{25,17},{2,10},{10... | collective-permute-start | bytes 4718600 | tf_op jit(solution)/shard_map/ppermute | solution.py:17
  654.7 42.5 %collective-permute-start.66 = (bf16[4,1,512,256]{3,2,1,0:T(8,128)(2,1)S(1)}, bf16[4,1,512,256]{3,2,1,0:T(8,128)(2,1)S(1)}, u32[]{:S(2)}, u32[]{:S(2)}) collective-permute-start(bf16[4,1,512,256]{3,2,1,0:T(8,128)(2,1)S(1)} %select_bitcast_fusion.8), channel_id=1, source_target_pairs={{0,16},{8,24},{16,0},{24,8},{1,17},{9,25},{17,1},{25,9},{2,18},{10... | collective-permute-start | bytes 3145736 | tf_op jit(solution)/shard_map/ppermute | solution.py:17
  674.2 47.2 %collective-permute-start.45 = (bf16[4,1,64,1536]{3,2,1,0:T(8,128)(2,1)S(1)}, bf16[4,1,64,1536]{3,2,1,0:T(8,128)(2,1)S(1)}, u32[]{:S(2)}, u32[]{:S(2)}) collective-permute-start(bf16[4,1,64,1536]{3,2,1,0:T(8,128)(2,1)S(1)} %select_bitcast_fusion.13), channel_id=1, source_target_pairs={{0,16},{8,24},{16,0},{24,8},{1,17},{9,25},{17,1},{25,9},{2,18},{10... | collective-permute-start | bytes 2359304 | tf_op jit(solution)/shard_map/ppermute | solution.py:17
  (107 other events, 1591.4 us)

commit v2 on v1

--- a/solution.py
+++ b/solution.py
@@ -25,58 +25,68 @@
     return jnp.stack([jnp.where(flag, theirs, mine), jnp.where(flag, mine, theirs)], dim)
 
 
-def gather_weight(block):
-    dp_count = lax.axis_size("dp")
+def after(done, values):
+    return lax.optimization_barrier((done, values))
+
+
+def cut_piece(block):
+    depth = block.shape[0] // lax.axis_size("dp")
+    piece = lax.dynamic_slice_in_dim(block, lax.axis_index("dp") * depth, depth, 0)
+    return piece.astype(jnp.bfloat16)
+
+
+def gather_col(piece):
     col_count = lax.axis_size("col")
-    depth = block.shape[0] // dp_count
-    piece = lax.dynamic_slice_in_dim(block, lax.axis_index("dp") * depth, depth, 0)
-    piece = piece.astype(jnp.bfloat16)
     parts = [piece] + [hop(piece, "col", k) for k in range(1, col_count)]
     step = 1
     while len(parts) > 1:
         flag = bit_of("col", step)
         parts = [in_order(parts[i], parts[i + 1], flag, 0) for i in range(0, len(parts), 2)]
         step *= 2
-    held = parts[0].reshape((col_count, 1) + piece.shape)
-    step = dp_count // 2
-    order = []
-    while step:
-        order.append(step)
-        step //= 2
-    for step in order:
-        pair = in_order(held, hop(held, "dp", step), bit_of("dp", step), 2)
-        held = pair.reshape((col_count, pair.shape[1] * 2) + piece.shape)
-    return held.reshape((col_count,) + block.shape)
-
-
-def reduce_weight(grad):
+    return parts[0].reshape((col_count, 1) + piece.shape)
+
+
+def gather_dp(held, step):
+    if step == 0:
+        return held
+    pair = in_order(held, hop(held, "dp", step), bit_of("dp", step), 2)
+    return pair.reshape((held.shape[0], held.shape[1] * 2) + held.shape[2:])
+
+
+def whole_block(held):
+    return held.reshape((held.shape[0], held.shape[1] * held.shape[2]) + held.shape[3:])
+
+
+def cut_grad(grad):
     dp_count = lax.axis_size("dp")
-    col_count = lax.axis_size("col")
-    depth = grad.shape[1] // dp_count
-    tail = grad.shape[2:]
-    held = grad.reshape((col_count, dp_count, depth) + tail)
-    step = 1
-    while step < dp_count:
-        pairs = held.reshape((col_count, held.shape[1] // 2, 2, depth) + tail)
-        flag = bit_of("dp", step)
-        keep = jnp.where(flag, pairs[:, :, 1], pairs[:, :, 0])
-        give = jnp.where(flag, pairs[:, :, 0], pairs[:, :, 1]).astype(jnp.bfloat16)
-        got = hop(give, "dp", step)
-        held = (keep.astype(jnp.float32) + got.astype(jnp.float32)).astype(jnp.bfloat16)
-        step *= 2
-    held = held[:, 0]
+    return grad.reshape((grad.shape[0], dp_count, grad.shape[1] // dp_count) + grad.shape[2:])
+
+
+def halve_dp(held, step):
+    pairs = held.reshape((held.shape[0], held.shape[1] // 2, 2) + held.shape[2:])
+    flag = bit_of("dp", step)
+    keep = jnp.where(flag, pairs[:, :, 1], pairs[:, :, 0])
+    give = jnp.where(flag, pairs[:, :, 0], pairs[:, :, 1])
+    got = hop(give, "dp", step)
+    return (keep.astype(jnp.float32) + got.astype(jnp.float32)).astype(jnp.bfloat16)
+
+
+def scatter_col(held):
     here = lax.axis_index("col")
     total = lax.dynamic_index_in_dim(held, here, 0, keepdims=False).astype(jnp.float32)
-    for k in range(1, col_count):
+    for k in range(1, held.shape[0]):
         give = lax.dynamic_index_in_dim(held, here ^ k, 0, keepdims=False)
         total = total + hop(give, "col", k).astype(jnp.float32)
-    out = total.astype(jnp.bfloat16)[None]
-    step = dp_count // 2
-    while step:
-        pair = in_order(out, hop(out, "dp", step), bit_of("dp", step), 1)
-        out = pair.reshape((pair.shape[0] * 2, depth) + tail)
-        step //= 2
-    return out.reshape((dp_count * depth,) + tail).astype(jnp.float32)
+    return total.astype(jnp.bfloat16)[None]
+
+
+def add_up(values, axes):
+    for axis in axes:
+        step = 1
+        while step < lax.axis_size(axis):
+            values = values + hop(values, axis, step)
+            step *= 2
+    return values
 
 
 def from_others(values):
@@ -159,6 +169,25 @@
     return parts[0]
 
 
+def gather_small(values):
+    parts, step = values, 1
+    while step < lax.axis_size("col"):
+        pair = in_order(parts, hop(parts, "col", step), bit_of("col", step), 1)
+        parts = pair.reshape(values.shape[0], -1)
+        step *= 2
+    return parts
+
+
+def outer_blocks(first, second):
+    width = second.shape[1] // lax.axis_size("col")
+    return jnp.stack(
+        [
+            outer(first, second[:, i * width : (i + 1) * width]).astype(jnp.bfloat16)
+            for i in range(lax.axis_size("col"))
+        ]
+    )
+
+
 def norm_forward(values, gain_row, shift_row):
     center = jnp.mean(values, -1, keepdims=True)
     spread = jnp.mean(values * values, -1, keepdims=True) - center * center
@@ -248,18 +277,23 @@
     gelu_exact = partial(jax.nn.gelu, approximate=False)
     rows, cols = lax.axis_size("row"), lax.axis_size("col")
     here_row, here_col = lax.axis_index("row"), lax.axis_index("col")
+    wide = w_qkv.shape[2]
+    far, near = lax.axis_size("dp") // 2, 1
+    qkv_held = gather_col(cut_piece(w_qkv.reshape(w_qkv.shape[0], 3 * wide)))
     own_tokens = to_tokens(tokens)
+    small = jnp.stack(
+        [out_bias, down_bias, norm_gain[0], norm_gain[1], norm_bias[0], norm_bias[1]]
+    )
+    small = gather_small(small)
+    qkv_held, (piece_out, piece_up) = after(qkv_held, (cut_piece(w_out), cut_piece(w_up)))
+    out_held, up_held = gather_col(piece_out), gather_col(piece_up)
     own_low = own_tokens.astype(jnp.bfloat16)
     other_low = from_others(own_low)
-    wide = w_qkv.shape[2]
-    w_qkv_all = gather_weight(w_qkv.reshape(w_qkv.shape[0], 3 * wide)).reshape(-1, 3 * wide)
-    w_out_all = gather_weight(w_out).transpose(1, 0, 2).reshape(w_out.shape[0], -1)
-    w_up_all = gather_weight(w_up).reshape(-1, w_up.shape[1])
-    w_down_all = gather_weight(w_down).transpose(1, 0, 2).reshape(w_down.shape[0], -1)
-    own_cotangent = to_tokens(cotangent)
-    small = jnp.concatenate([out_bias, down_bias, norm_gain[0], norm_gain[1], norm_bias[0], norm_bias[1]])
-    small = lax.all_gather(small, "col", axis=0).reshape(cols, 6, -1)
-    small = small.transpose(1, 0, 2).reshape(6, -1)
+    qkv_held, piece_down = after(gather_dp(qkv_held, far), cut_piece(w_down))
+    down_held = gather_col(piece_down)
+    qkv_held, (out_held, up_held) = after(gather_dp(qkv_held, near), (out_held, up_held))
+    w_qkv_all = whole_block(qkv_held).reshape(-1, 3 * wide)
+    out_held, up_held = gather_dp(out_held, far), gather_dp(up_held, far)
     out_bias_all, down_bias_all = small[0], small[1]
     gains, shifts = small[2:4], small[4:6]
 
@@ -272,6 +306,9 @@
         ],
         0,
     )
+    qkv, (out_held, up_held, down_held) = after(qkv, (out_held, up_held, down_held))
+    out_held, down_held = gather_dp(out_held, near), gather_dp(down_held, far)
+    up_held = gather_dp(up_held, near)
     length = qkv.shape[0]
     head_count = wide // HD
     qkv = qkv.reshape(length, 3, head_count, HD)
@@ -282,47 +319,61 @@
     same_seq = (segment[:, None] == segment[None, :])[None]
     context, log_total = attend(query_rows, key_rows, value_rows, same_seq, score_scale)
     context = context.reshape(length, wide).astype(jnp.bfloat16)
+    context, (down_held, cotangent) = after(context, (down_held, cotangent))
+    w_out_all = whole_block(out_held).transpose(1, 0, 2).reshape(w_out.shape[0], -1)
+    down_held = gather_dp(down_held, near)
     attn_other = dot(context[size:], w_out_all)
     attn_out = to_owners(attn_other, dot(context[:size], w_out_all)) + out_bias_all
     normed_one, normal_one, inv_one = norm_forward(own_tokens + attn_out, gains[0], shifts[0])
     normed_own = normed_one.astype(jnp.bfloat16)
+    normed_own, cotangent = after(normed_own, cotangent)
     normed_other = from_others(normed_own)
+    own_cotangent = to_tokens(cotangent)
+    w_up_all = whole_block(up_held).reshape(-1, w_up.shape[1])
+    w_down_all = whole_block(down_held).transpose(1, 0, 2).reshape(w_down.shape[0], -1)
     pre_own = dot(normed_own, w_up_all) + up_bias
     pre_other = dot(normed_other, w_up_all) + up_bias
     hidden_own = gelu_exact(pre_own).astype(jnp.bfloat16)
     hidden_other = gelu_exact(pre_other).astype(jnp.bfloat16)
+    hidden = jnp.concatenate([hidden_own, hidden_other], 0)
     mlp_other = dot(hidden_other, w_down_all)
     mlp_out = to_owners(mlp_other, dot(hidden_own, w_down_all)) + down_bias_all
     last, normal_two, inv_two = norm_forward(normed_one + mlp_out, gains[1], shifts[1])
-    output = from_tokens(last)
     grad_last = norm_backward(own_cotangent, normal_two, inv_two, gains[1])
     gain_two = jnp.sum(own_cotangent * normal_two, 0)
     shift_two = jnp.sum(own_cotangent, 0)
     mlp_grad_own = grad_last.astype(jnp.bfloat16)
     mlp_grad_other = from_others(mlp_grad_own)
     down_total = jnp.sum(mlp_grad_own, 0, dtype=jnp.float32)
+    mlp_grad_own, last = after(mlp_grad_own, last)
+    output = from_tokens(last)
+    down_sum = cut_grad(outer_blocks(hidden, jnp.concatenate([mlp_grad_own, mlp_grad_other], 0)))
+    down_sum = halve_dp(down_sum, near)
     pre_grad_own = jax.vjp(gelu_exact, pre_own)[1](dot_back(mlp_grad_own, w_down_all))[0]
     pre_grad_own = pre_grad_own.astype(jnp.bfloat16)
     pre_grad_other = jax.vjp(gelu_exact, pre_other)[1](dot_back(mlp_grad_other, w_down_all))[0]
     pre_grad_other = pre_grad_other.astype(jnp.bfloat16)
+    pre_grad_other, down_sum = after(pre_grad_other, down_sum)
+    down_sum = halve_dp(down_sum, far)
     normed_part = dot_back(pre_grad_other, w_up_all)
     grad_normed = to_owners(normed_part, dot_back(pre_grad_own, w_up_all)) + grad_last
     pre_grad = jnp.concatenate([pre_grad_own, pre_grad_other], 0)
     up_total = jnp.sum(pre_grad, 0, dtype=jnp.float32)
-    down_grad = outer(
-        jnp.concatenate([hidden_own, hidden_other], 0),
-        jnp.concatenate([mlp_grad_own, mlp_grad_other], 0),
-    )
-    down_grad = down_grad.astype(jnp.bfloat16).reshape(w_down.shape[0], cols, -1).transpose(1, 0, 2)
-    grad_w_down = reduce_weight(down_grad)
     up_grad = outer(jnp.concatenate([normed_own, normed_other], 0), pre_grad).astype(jnp.bfloat16)
-    grad_w_up = reduce_weight(up_grad.reshape((cols,) + w_up.shape))
+    up_sum = halve_dp(cut_grad(up_grad.reshape((cols,) + w_up.shape)), near)
     grad_middle = norm_backward(grad_normed, normal_one, inv_one, gains[0])
     gain_one = jnp.sum(grad_normed * normal_one, 0)
     shift_one = jnp.sum(grad_normed, 0)
     attn_grad_own = grad_middle.astype(jnp.bfloat16)
+    attn_grad_own, (down_sum, up_sum) = after(attn_grad_own, (down_sum, up_sum))
     attn_grad_other = from_others(attn_grad_own)
+    down_sum = scatter_col(down_sum)
+    up_sum = halve_dp(up_sum, far)
     out_total = jnp.sum(attn_grad_own, 0, dtype=jnp.float32)
+    totals = add_up(
+        jnp.stack([out_total, down_total, gain_one, gain_two, shift_one, shift_two]),
+        ("row", "col", "dp"),
+    )
     grad_context = jnp.concatenate(
         [
             dot_back(attn_grad_own, w_out_all).astype(jnp.bfloat16),
@@ -330,9 +381,8 @@
         ],
         0,
     ).reshape(length, head_count, HD)
-    out_grad = outer(context, jnp.concatenate([attn_grad_own, attn_grad_other], 0))
-    out_grad = out_grad.astype(jnp.bfloat16).reshape(w_out.shape[0], cols, -1).transpose(1, 0, 2)
-    grad_w_out = reduce_weight(out_grad)
+    attn_grad = jnp.concatenate([attn_grad_own, attn_grad_other], 0)
+    out_sum = halve_dp(cut_grad(outer_blocks(context, attn_grad)), near)
     grad_queries, grad_keys, grad_values = attend_back(
         query_rows, key_rows, value_rows, same_seq, score_scale, log_total, grad_context
     )
@@ -341,33 +391,49 @@
         .reshape(length, 3 * wide)
         .astype(jnp.bfloat16)
     )
+    grad_qkv, (down_sum, up_sum, out_sum) = after(grad_qkv, (down_sum, up_sum, out_sum))
     qkv_totals = jnp.sum(grad_qkv, 0, dtype=jnp.float32)
     qkv_grad = outer(jnp.concatenate([own_low, other_low], 0), grad_qkv).astype(jnp.bfloat16)
-    grad_w_qkv = reduce_weight(qkv_grad.reshape(cols, -1, 3 * wide)).reshape(w_qkv.shape)
+    qkv_sum = halve_dp(cut_grad(qkv_grad.reshape(cols, -1, 3 * wide)), near)
+    out_sum = halve_dp(out_sum, far)
+    up_sum = scatter_col(up_sum)
+    down_sum = gather_dp(down_sum, far)
     input_other = dot_back(grad_qkv[size:], w_qkv_all)
+    halves = add_up(
+        jnp.concatenate([up_total, qkv_totals[:wide], qkv_totals[2 * wide :]])[None],
+        ("col", "dp"),
+    )[0]
     grad_own = to_owners(input_other, dot_back(grad_qkv[:size], w_qkv_all)) + grad_middle
+    qkv_sum, (out_sum, up_sum, down_sum, grad_own) = after(
+        qkv_sum, (out_sum, up_sum, down_sum, grad_own)
+    )
+    qkv_sum = halve_dp(qkv_sum, far)
     grad_input = from_tokens(grad_own)
-
-    everywhere = lax.psum(
-        jnp.stack([out_total, down_total, gain_one, gain_two, shift_one, shift_two]),
-        ("dp", "row", "col"),
-    )
-    part = everywhere.shape[1] // cols
-    mine = lax.dynamic_slice_in_dim(everywhere, here_col * part, part, 1)
-    halves = lax.psum(
-        jnp.concatenate([up_total, qkv_totals[:wide], qkv_totals[2 * wide :]]), ("dp", "col")
-    )
+    out_sum = scatter_col(out_sum)
+    up_sum = gather_dp(up_sum, far)
+    down_sum = gather_dp(down_sum, near)
+    qkv_sum, (out_sum, up_sum) = after(qkv_sum, (out_sum, up_sum))
+    qkv_sum = scatter_col(qkv_sum)
+    out_sum = gather_dp(out_sum, far)
+    up_sum = gather_dp(up_sum, near)
+    qkv_sum, out_sum = after(qkv_sum, out_sum)
+    qkv_sum = gather_dp(qkv_sum, far)
+    out_sum = gather_dp(out_sum, near)
+    qkv_sum = gather_dp(qkv_sum, near)
+
+    part = totals.shape[1] // cols
+    mine = lax.dynamic_slice_in_dim(totals, here_col * part, part, 1)
     hid = up_total.shape[0]
     return (
         output,
         grad_input,
-        grad_w_qkv,
+        whole_block(qkv_sum)[0].astype(jnp.float32).reshape(w_qkv.shape),
         halves[hid:].reshape(2, wide),
-        grad_w_out,
+        whole_block(out_sum)[0].astype(jnp.float32),
         mine[0],
-        grad_w_up,
+        whole_block(up_sum)[0].astype(jnp.float32),
         halves[:hid],
-        grad_w_down,
+        whole_block(down_sum)[0].astype(jnp.float32),
         mine[1],
         mine[2:4],
         mine[4:6],

time: 778 us -> 657 us (0.84)
  blocking collectives: 119 us -> 0 us
  waiting for transfers between devices: 192 us -> 257 us
  local copies, waits for them, and re-layouts: 81.2 us -> 44.1 us
  other arithmetic: 75.6 us -> 60.5 us
    psum x2 -> x0, blocking collectives: 107 us -> none  [the longest x1 58.3 us: shards(): lax.psum(jnp.concatenate([up_total, qkv_totals[:wide], qkv_totals[2 * wid...]
    ppermute x48 -> x59, waiting for transfers between devices: 99.4 us -> 169 us  [hop(): return lax.ppermute(values, axis, [(i, i ^ step) for i in range(count)])]
    ppermute x48 -> x59, starting transfers between devices: 116 us -> 149 us  [hop(): return lax.ppermute(values, axis, [(i, i ^ step) for i in range(count)])]
    ppermute x8, waiting for transfers between devices: 30.7 us -> 55.7 us  [to_tokens(): got.append(lax.ppermute(give, ('row', 'col'), owner_perm(rows, cols, k)))]
    ppermute x8, starting transfers between devices: 41.1 us -> 20.7 us  [from_tokens(): got.append(lax.ppermute(give, ('row', 'col'), back))]
    unnamed x126 -> x146, local copies, waits for them, and re-layouts: 32 us -> 13.2 us
    ppermute x4, waiting for transfers between devices: 28.6 us -> 14.9 us  [to_owners(): lax.ppermute(low[(k - 1) * size:k * size], 'row', [(i, (i + k) % count) f...]
    all_gather x1 -> x0, blocking collectives: 12.2 us -> none  [shards(): small = lax.all_gather(small, 'col', axis=0).reshape(cols, 6, -1)]
  transfers between devices with their start and end apart: 72 -> 83, of which waited for: 17 -> 34; matrix products, arithmetic and copies ran while one was open for 25% -> 22% of each run, Pallas kernels for 0% -> 0%
where the time goes in v2:
time: 657 us; the launch traced here: 650 us
  waiting for transfers between devices  257 us (39%)
  starting transfers between devices  202 us (31%)
  matrix products  82.6 us (13%)
  other arithmetic  60.5 us (9%)
  local copies, waits for them, and re-layouts  44.1 us (7%)
    ppermute x59, waiting for transfers between devices, hop(): return lax.ppermute(values, axis, [(i, i ^ step) for i in range(count)])  169 us
    ppermute x59, starting transfers between devices, hop(): return lax.ppermute(values, axis, [(i, i ^ step) for i in range(count)])  149 us
    ppermute x8, waiting for transfers between devices, to_tokens(): got.append(lax.ppermute(give, ('row', 'col'), owner_perm(rows, cols, k)))  55.7 us
    dot_general x8, matrix products, dot(): return jnp.dot(first, second, preferred_element_type=jnp.float32)  28.9 us
    ppermute x8, starting transfers between devices, to_tokens(): got.append(lax.ppermute(give, ('row', 'col'), owner_perm(rows, cols, k)))  22.2 us
    ppermute x8, starting transfers between devices, from_tokens(): got.append(lax.ppermute(give, ('row', 'col'), back))  20.7 us
    another operation x42, other arithmetic, in_order(): jnp.stack([jnp.where(flag, theirs, mine), jnp.where(flag, mine, theirs)],...  16.9 us
    dot_general x10, matrix products, outer(): jnp.einsum('td,tf->df', first, second, preferred_element_type=jnp.float32)  15.6 us
  transfers between devices with their start and end apart: 83, of which 34 were waited for; matrix products, arithmetic and copies ran while one was open for 22% of the time, Pallas kernels for 0%

profile of v2, /device:TPU:1, one launch (start us, length us, event | category | flops | bytes accessed | tf_op | source)
XLA Modules:
  0.0 649.8 jit_solution(9309693471348560540)
XLA Ops:
  35.5 22.7 %collective-permute-start.11 = (bf16[128,256]{1,0:T(8,128)(2,1)S(1)}, bf16[128,256]{1,0:T(8,128)(2,1)S(1)}, u32[]{:S(2)}, u32[]{:S(2)}) collective-permute-start(bf16[128,256]{1,0:T(8,128)(2,1)S(1)} %dynamic-slice_convert_fusion.3), channel_id=1, source_target_pairs={{0,1},{1,0},{2,3},{3,2},{4,5},{5,4},{6,7},{7,6},{8,9},{9,8},{10,11... | collective-permute-start | bytes 196616 | tf_op jit(solution)/shard_map/ppermute | solution.py:17
  62.2 25.7 %collective-permute-done.10 = bf16[128,256]{1,0:T(8,128)(2,1)S(1)} collective-permute-done((bf16[128,256]{1,0:T(8,128)(2,1)S(1)}, bf16[128,256]{1,0:T(8,128)(2,1)S(1)}, u32[]{:S(2)}, u32[]{:S(2)}) %collective-permute-start.10) | collective-permute-done | bytes 65568 | tf_op jit(solution)/shard_map/ppermute | solution.py:17
  107.8 7.3 %collective-permute-done.7 = bf16[4,1,64,1536]{3,2,0,1:T(8,128)(2,1)S(1)} collective-permute-done((bf16[4,1,64,1536]{3,2,0,1:T(8,128)(2,1)S(1)}, bf16[4,1,64,1536]{3,2,0,1:T(8,128)(2,1)S(1)}, u32[]{:S(2)}, u32[]{:S(2)}) %collective-permute-start.7) | collective-permute-done | bytes 786464 | tf_op jit(solution)/shard_map/ppermute | solution.py:17
  115.5 17.3 %collective-permute-start.8 = (bf16[4,2,64,1536]{3,2,1,0:T(8,128)(2,1)S(1)}, bf16[4,2,64,1536]{3,2,1,0:T(8,128)(2,1)S(1)}, u32[]{:S(2)}, u32[]{:S(2)}) collective-permute-start(bf16[4,2,64,1536]{3,2,1,0:T(8,128)(2,1)S(1)} %maximum_bitcast_fusion.2), channel_id=1, source_target_pairs={{0,8},{8,0},{16,24},{24,16},{1,9},{9,1},{17,25},{25,17},{2,10},{10... | collective-permute-start | bytes 4718600 | tf_op jit(solution)/shard_map/ppermute | solution.py:17
  136.8 7.1 %collective-permute-done.20 = bf16[512,256]{1,0:T(8,128)(2,1)S(1)} collective-permute-done((bf16[512,256]{1,0:T(8,128)(2,1)S(1)}, bf16[512,256]{1,0:T(8,128)(2,1)S(1)}, u32[]{:S(2)}, u32[]{:S(2)}) %collective-permute-start.20) | collective-permute-done | bytes 262176 | tf_op jit(solution)/shard_map/ppermute | solution.py:17
  163.7 18.6 %collective-permute-done.17 = bf16[4,1,64,2048]{3,2,0,1:T(8,128)(2,1)S(1)} collective-permute-done((bf16[4,1,64,2048]{3,2,0,1:T(8,128)(2,1)S(1)}, bf16[4,1,64,2048]{3,2,0,1:T(8,128)(2,1)S(1)}, u32[]{:S(2)}, u32[]{:S(2)}) %collective-permute-start.17) | collective-permute-done | bytes 1048608 | tf_op jit(solution)/shard_map/ppermute | solution.py:17
  203.7 11.6 %collective-permute-done.21 = bf16[4,1,512,256]{3,2,0,1:T(8,128)(2,1)} collective-permute-done((bf16[4,1,512,256]{3,2,0,1:T(8,128)(2,1)}, bf16[4,1,512,256]{3,2,0,1:T(8,128)(2,1)}, u32[]{:S(2)}, u32[]{:S(2)}) %collective-permute-start.21) | collective-permute-done | bytes 1048608 | tf_op jit(solution)/shard_map/ppermute | solution.py:17
  222.8 7.1 %collective-permute-start.25 = (f32[6,512]{1,0:T(8,128)S(1)}, f32[6,512]{1,0:T(8,128)S(1)}, u32[]{:S(2)}, u32[]{:S(2)}) collective-permute-start(f32[6,512]{1,0:T(8,128)S(1)} %bitcast.570), channel_id=1, source_target_pairs={{0,2},{1,3},{2,0},{3,1},{4,6},{5,7},{6,4},{7,5},{8,10},{9,11},{10,... | collective-permute-start | bytes 36872 | tf_op jit(solution)/shard_map/ppermute | solution.py:17
  240.4 9.5 %collective-permute-start.32 = (f32[320,256]{1,0:T(8,128)S(1)}, f32[320,256]{1,0:T(8,128)S(1)}, u32[]{:S(2)}, u32[]{:S(2)}) collective-permute-start(f32[320,256]{1,0:T(8,128)S(1)} %get-tuple-element.168), channel_id=1, source_target_pairs={{0,4},{1,0},{2,5},{3,1},{4,6},{5,2},{6,7},{7,3},{8,12},{9,8},{10,1... | collective-permute-start | bytes 983048 | tf_op jit(solution)/shard_map/ppermute | solution.py:133
  254.4 7.4 %collective-permute-done.32 = f32[320,256]{1,0:T(8,128)S(1)} collective-permute-done((f32[320,256]{1,0:T(8,128)S(1)}, f32[320,256]{1,0:T(8,128)S(1)}, u32[]{:S(2)}, u32[]{:S(2)}) %collective-permute-start.32) | collective-permute-done | bytes 327712 | tf_op jit(solution)/shard_map/ppermute | solution.py:133
  264.0 7.9 %collective-permute-done.30 = f32[320,256]{1,0:T(8,128)S(1)} collective-permute-done((f32[320,256]{1,0:T(8,128)S(1)}, f32[320,256]{1,0:T(8,128)S(1)}, u32[]{:S(2)}, u32[]{:S(2)}) %collective-permute-start.30) | collective-permute-done | bytes 327712 | tf_op jit(solution)/shard_map/ppermute | solution.py:133
  272.0 32.3 %collective-permute-done.31 = f32[320,256]{1,0:T(8,128)S(1)} collective-permute-done((f32[320,256]{1,0:T(8,128)S(1)}, f32[320,256]{1,0:T(8,128)S(1)}, u32[]{:S(2)}, u32[]{:S(2)}) %collective-permute-start.31) | collective-permute-done | bytes 327712 | tf_op jit(solution)/shard_map/ppermute | solution.py:133
  306.8 8.7 %multiply_convert_fusion.1 = (bf16[320,2048]{1,0:T(8,128)(2,1)}, f32[320,2048]{1,0:T(8,128)}, f32[320,2048]{1,0:T(8,128)}) fusion(f32[2048]{0:T(1024)S(1)} %copy-done.58, bf16[320,1024]{1,0:T(8,128)(2,1)S(1)} %collective-permute-done.28, bf16[1024,2048]{1,0:T(8,128)(2,1)S(1)} %bitcast.523), kind=kOutput, calls=%fused_computation.41 | convolution fusion | flops 1385431040 | bytes 11411456 | tf_op jit(solution)/shard_map/dot_general | solution.py:207
  328.9 8.5 %multiply_convert_fusion.2 = (bf16[320,2048]{1,0:T(8,128)(2,1)S(1)}, f32[320,2048]{1,0:T(8,128)}, f32[320,2048]{1,0:T(8,128)}) fusion(f32[2048]{0:T(1024)S(1)} %copy-done.58, bf16[320,1024]{1,0:T(8,128)(2,1)S(1)} %copy-done.40, bf16[1024,2048]{1,0:T(8,128)(2,1)S(1)} %bitcast.524), kind=kOutput, calls=%fused_computation.54 | convolution fusion | flops 1385431040 | bytes 11411456 | tf_op jit(solution)/shard_map/dot_general | solution.py:207
  349.2 6.5 %collective-permute-start.34 = (f32[320,256]{1,0:T(8,128)S(1)}, f32[320,256]{1,0:T(8,128)S(1)}, u32[]{:S(2)}, u32[]{:S(2)}) collective-permute-start(f32[320,256]{1,0:T(8,128)S(1)} %get-tuple-element.160), channel_id=1, source_target_pairs={{5,0},{1,1},{4,2},{0,3},{7,4},{3,5},{6,6},{2,7},{13,8},{9,9},{12,1... | collective-permute-start | bytes 983048 | tf_op jit(solution)/shard_map/ppermute | solution.py:160
  371.1 10.4 %collective-permute-start.39 = (bf16[4,2,512,256]{3,2,1,0:T(8,128)(2,1)S(1)}, bf16[4,2,512,256]{3,2,1,0:T(8,128)(2,1)S(1)}, u32[]{:S(2)}, u32[]{:S(2)}) collective-permute-start(bf16[4,2,512,256]{3,2,1,0:T(8,128)(2,1)S(1)} %fusion.23), channel_id=1, source_target_pairs={{0,8},{8,0},{16,24},{24,16},{1,9},{9,1},{17,25},{25,17},{2,10},{10... | collective-permute-start | bytes 6291464 | tf_op jit(solution)/shard_map/ppermute | solution.py:17
  407.8 17.3 %collective-permute-done.41 = bf16[4,1,512,256]{3,2,0,1:T(8,128)(2,1)S(1)} collective-permute-done((bf16[4,1,512,256]{3,2,0,1:T(8,128)(2,1)S(1)}, bf16[4,1,512,256]{3,2,0,1:T(8,128)(2,1)S(1)}, u32[]{:S(2)}, u32[]{:S(2)}) %collective-permute-start.41) | collective-permute-done | bytes 1048608 | tf_op jit(solution)/shard_map/ppermute | solution.py:17
  467.2 12.2 %multiply_reduce_fusion = (f32[8,640]{1,0:T(8,128)S(1)}, f32[8,640,640]{1,2,0:T(8,128)}) fusion(f32[8,640,640]{1,2,0:T(8,128)} %copy-done.2, f32[8,640]{1,0:T(8,128)S(1)} %log_add_fusion, bf16[640,8,64]{0,2,1:T(8,128)(2,1)S(1)} %bitcast.517, bf16[640,3,8,64]{0,3,2,1:T(8,128)(2,1)} %bitcast.507), kind=kOutput, calls=%fused_computation.1 | convolution fusion | flops 429255680 | bytes 27566080 | tf_op jit(solution)/shard_map/qhe,khe->hqk/dot_general | solution.py:239
  479.4 6.7 %multiply_convert_fusion = bf16[8,640,640]{1,2,0:T(8,128)(2,1)S(1)} fusion(f32[8,640,640]{1,2,0:T(8,128)} %get-tuple-element.274, f32[8,640,640]{1,2,0:T(8,128)S(1)} %bitcast.497, f32[8,640]{1,0:T(8,128)S(1)} %get-tuple-element.273, f32[8,640]{1,0:T(8,128)S(1)} %log_add_fusion), kind=kLoop, calls=%fused_computation | loop fusion | flops 13107200 | bytes 32808960 | tf_op jit(solution)/shard_map/convert_element_type | solution.py:249
  536.1 16.3 %collective-permute-done.52 = bf16[1,64,2048]{2,1,0:T(8,128)(2,1)S(1)} collective-permute-done((bf16[1,64,2048]{2,1,0:T(8,128)(2,1)}, bf16[1,64,2048]{2,1,0:T(8,128)(2,1)S(1)}, u32[]{:S(2)}, u32[]{:S(2)}) %collective-permute-start.52) | collective-permute-done | bytes 262176 | tf_op jit(solution)/shard_map/ppermute | solution.py:17
  586.5 8.6 %collective-permute-done.60 = bf16[4,1,64,1536]{3,2,1,0:T(8,128)(2,1)S(1)} collective-permute-done((bf16[4,1,64,1536]{3,2,1,0:T(8,128)(2,1)S(1)}, bf16[4,1,64,1536]{3,2,1,0:T(8,128)(2,1)S(1)}, u32[]{:S(2)}, u32[]{:S(2)}) %collective-permute-start.60) | collective-permute-done | bytes 786464 | tf_op jit(solution)/shard_map/ppermute | solution.py:17
  598.1 12.9 %collective-permute-start.67 = (bf16[1,64,1536]{2,1,0:T(8,128)(2,1)S(1)}, bf16[1,64,1536]{2,1,0:T(8,128)(2,1)S(1)}, u32[]{:S(2)}, u32[]{:S(2)}) collective-permute-start(bf16[1,64,1536]{2,1,0:T(8,128)(2,1)S(1)} %get-tuple-element.195), channel_id=1, source_target_pairs={{0,3},{1,2},{2,1},{3,0},{4,7},{5,6},{6,5},{7,4},{8,11},{9,10},{10,... | collective-permute-start | bytes 589832 | tf_op jit(solution)/shard_map/ppermute | solution.py:17
  611.2 6.5 %collective-permute-done.67 = bf16[1,64,1536]{2,1,0:T(8,128)(2,1)S(1)} collective-permute-done((bf16[1,64,1536]{2,1,0:T(8,128)(2,1)S(1)}, bf16[1,64,1536]{2,1,0:T(8,128)(2,1)S(1)}, u32[]{:S(2)}, u32[]{:S(2)}) %collective-permute-start.67) | collective-permute-done | bytes 196640 | tf_op jit(solution)/shard_map/ppermute | solution.py:17
  617.7 9.1 %collective-permute-done.66 = bf16[1,64,1536]{2,1,0:T(8,128)(2,1)S(1)} collective-permute-done((bf16[1,64,1536]{2,1,0:T(8,128)(2,1)S(1)}, bf16[1,64,1536]{2,1,0:T(8,128)(2,1)S(1)}, u32[]{:S(2)}, u32[]{:S(2)}) %collective-permute-start.66) | collective-permute-done | bytes 196640 | tf_op jit(solution)/shard_map/ppermute | solution.py:17
  (478 shorter events, 348.3 us)
Async XLA Ops:
  7.9 25.7 %collective-permute-start.4 = (bf16[64,1536]{0,1:T(8,128)(2,1)}, bf16[64,1536]{0,1:T(8,128)(2,1)}, u32[]{:S(2)}, u32[]{:S(2)}) collective-permute-start(bf16[64,1536]{0,1:T(8,128)(2,1)} %dynamic-slice_convert_fusion), channel_id=1, source_target_pairs={{0,3},{1,2},{2,1},{3,0},{4,7},{5,6},{6,5},{7,4},{8,11},{9,10},{10,... | collective-permute-start | bytes 589832 | tf_op jit(solution)/shard_map/ppermute | solution.py:17
  8.0 214.8 %collective-permute-start.24 = (f32[6,256]{1,0:T(8,128)S(1)}, f32[6,256]{1,0:T(8,128)S(1)}, u32[]{:S(2)}, u32[]{:S(2)}) collective-permute-start(f32[6,256]{1,0:T(8,128)S(1)} %pad_maximum_fusion.39), channel_id=1, source_target_pairs={{0,1},{1,0},{2,3},{3,2},{4,5},{5,4},{6,7},{7,6},{8,9},{9,8},{10,11... | collective-permute-start | bytes 18440 | tf_op jit(solution)/shard_map/ppermute | solution.py:17
  10.7 89.2 %collective-permute-start = (f32[320,256]{1,0:T(8,128)}, f32[320,256]{1,0:T(8,128)}, u32[]{:S(2)}, u32[]{:S(2)}) collective-permute-start(f32[320,256]{1,0:T(8,128)} %get-tuple-element.172), channel_id=1, source_target_pairs={{0,5},{1,1},{2,4},{3,0},{4,7},{5,3},{6,6},{7,2},{8,13},{9,9},{10,1... | collective-permute-start | bytes 983048 | tf_op jit(solution)/shard_map/ppermute | solution.py:133
  22.4 67.7 %collective-permute-start.3 = (f32[320,256]{1,0:T(8,128)}, f32[320,256]{1,0:T(8,128)}, u32[]{:S(2)}, u32[]{:S(2)}) collective-permute-start(f32[320,256]{1,0:T(8,128)} %get-tuple-element.173), channel_id=1, source_target_pairs={{0,0},{1,4},{2,1},{3,5},{4,2},{5,6},{6,3},{7,7},{8,8},{9,12},{10,9... | collective-permute-start | bytes 983048 | tf_op jit(solution)/shard_map/ppermute | solution.py:133
  35.5 26.6 %collective-permute-start.11 = (bf16[128,256]{1,0:T(8,128)(2,1)S(1)}, bf16[128,256]{1,0:T(8,128)(2,1)S(1)}, u32[]{:S(2)}, u32[]{:S(2)}) collective-permute-start(bf16[128,256]{1,0:T(8,128)(2,1)S(1)} %dynamic-slice_convert_fusion.3), channel_id=1, source_target_pairs={{0,1},{1,0},{2,3},{3,2},{4,5},{5,4},{6,7},{7,6},{8,9},{9,8},{10,11... | collective-permute-start | bytes 196616 | tf_op jit(solution)/shard_map/ppermute | solution.py:17
  58.3 29.6 %collective-permute-start.10 = (bf16[128,256]{1,0:T(8,128)(2,1)S(1)}, bf16[128,256]{1,0:T(8,128)(2,1)S(1)}, u32[]{:S(2)}, u32[]{:S(2)}) collective-permute-start(bf16[128,256]{1,0:T(8,128)(2,1)S(1)} %dynamic-slice_convert_fusion.3), channel_id=1, source_target_pairs={{0,2},{1,3},{2,0},{3,1},{4,6},{5,7},{6,4},{7,5},{8,10},{9,11},{10,... | collective-permute-start | bytes 196616 | tf_op jit(solution)/shard_map/ppermute | solution.py:17
  62.2 25.7 %collective-permute-start.9 = (bf16[128,256]{1,0:T(8,128)(2,1)S(1)}, bf16[128,256]{1,0:T(8,128)(2,1)S(1)}, u32[]{:S(2)}, u32[]{:S(2)}) collective-permute-start(bf16[128,256]{1,0:T(8,128)(2,1)S(1)} %dynamic-slice_convert_fusion.3), channel_id=1, source_target_pairs={{0,3},{1,2},{2,1},{3,0},{4,7},{5,6},{6,5},{7,4},{8,11},{9,10},{10,... | collective-permute-start | bytes 196616 | tf_op jit(solution)/shard_map/ppermute | solution.py:17
  94.3 38.5 %collective-permute-start.13 = (bf16[64,2048]{1,0:T(8,128)(2,1)}, bf16[64,2048]{1,0:T(8,128)(2,1)S(1)}, u32[]{:S(2)}, u32[]{:S(2)}) collective-permute-start(bf16[64,2048]{1,0:T(8,128)(2,1)} %dynamic-slice_convert_fusion.2), channel_id=1, source_target_pairs={{0,2},{1,3},{2,0},{3,1},{4,6},{5,7},{6,4},{7,5},{8,10},{9,11},{10,... | collective-permute-start | bytes 786440 | tf_op jit(solution)/shard_map/ppermute | solution.py:17
  99.9 32.9 %collective-permute-start.12 = (bf16[64,2048]{1,0:T(8,128)(2,1)}, bf16[64,2048]{1,0:T(8,128)(2,1)S(1)}, u32[]{:S(2)}, u32[]{:S(2)}) collective-permute-start(bf16[64,2048]{1,0:T(8,128)(2,1)} %dynamic-slice_convert_fusion.2), channel_id=1, source_target_pairs={{0,3},{1,2},{2,1},{3,0},{4,7},{5,6},{6,5},{7,4},{8,11},{9,10},{10,... | collective-permute-start | bytes 786440 | tf_op jit(solution)/shard_map/ppermute | solution.py:17
  115.5 38.4 %collective-permute-start.8 = (bf16[4,2,64,1536]{3,2,1,0:T(8,128)(2,1)S(1)}, bf16[4,2,64,1536]{3,2,1,0:T(8,128)(2,1)S(1)}, u32[]{:S(2)}, u32[]{:S(2)}) collective-permute-start(bf16[4,2,64,1536]{3,2,1,0:T(8,128)(2,1)S(1)} %maximum_bitcast_fusion.2), channel_id=1, source_target_pairs={{0,8},{8,0},{16,24},{24,16},{1,9},{9,1},{17,25},{25,17},{2,10},{10... | collective-permute-start | bytes 4718600 | tf_op jit(solution)/shard_map/ppermute | solution.py:17
  155.7 26.6 %collective-permute-start.17 = (bf16[4,1,64,2048]{3,2,0,1:T(8,128)(2,1)S(1)}, bf16[4,1,64,2048]{3,2,0,1:T(8,128)(2,1)S(1)}, u32[]{:S(2)}, u32[]{:S(2)}) collective-permute-start(bf16[4,1,64,2048]{3,2,0,1:T(8,128)(2,1)S(1)} %bitcast.521), channel_id=1, source_target_pairs={{0,16},{8,24},{16,0},{24,8},{1,17},{9,25},{17,1},{25,9},{2,18},{10... | collective-permute-start | bytes 3145736 | tf_op jit(solution)/shard_map/ppermute | solution.py:17
  229.9 75.7 %collective-permute-start.26 = (bf16[4,2,64,2048]{3,2,1,0:T(8,128)(2,1)S(1)}, bf16[4,2,64,2048]{3,2,1,0:T(8,128)(2,1)S(1)}, u32[]{:S(2)}, u32[]{:S(2)}) collective-permute-start(bf16[4,2,64,2048]{3,2,1,0:T(8,128)(2,1)S(1)} %copy-done.7), channel_id=1, source_target_pairs={{0,8},{8,0},{16,24},{24,16},{1,9},{9,1},{17,25},{25,17},{2,10},{10... | collective-permute-start | bytes 6291464 | tf_op jit(solution)/shard_map/ppermute | solution.py:17
  252.0 52.3 %collective-permute-start.31 = (f32[320,256]{1,0:T(8,128)S(1)}, f32[320,256]{1,0:T(8,128)S(1)}, u32[]{:S(2)}, u32[]{:S(2)}) collective-permute-start(f32[320,256]{1,0:T(8,128)S(1)} %get-tuple-element.169), channel_id=1, source_target_pairs={{0,1},{1,5},{2,0},{3,4},{4,3},{5,7},{6,2},{7,6},{8,9},{9,13},{10,8... | collective-permute-start | bytes 983048 | tf_op jit(solution)/shard_map/ppermute | solution.py:133
  252.0 63.5 %collective-permute-start.27 = (bf16[4,2,512,256]{3,2,1,0:T(8,128)(2,1)S(1)}, bf16[4,2,512,256]{3,2,1,0:T(8,128)(2,1)S(1)}, u32[]{:S(2)}, u32[]{:S(2)}) collective-permute-start(bf16[4,2,512,256]{3,2,1,0:T(8,128)(2,1)S(1)} %maximum_bitcast_fusion.1), channel_id=1, source_target_pairs={{0,8},{8,0},{16,24},{24,16},{1,9},{9,1},{17,25},{25,17},{2,10},{10... | collective-permute-start | bytes 6291464 | tf_op jit(solution)/shard_map/ppermute | solution.py:17
  261.8 44.7 %collective-permute-start.28 = (bf16[320,1024]{1,0:T(8,128)(2,1)S(1)}, bf16[320,1024]{1,0:T(8,128)(2,1)S(1)}, u32[]{:S(2)}, u32[]{:S(2)}) collective-permute-start(bf16[320,1024]{1,0:T(8,128)(2,1)S(1)} %fusion.52), channel_id=1, source_target_pairs={{4,0},{0,4},{5,1},{1,5},{6,2},{2,6},{7,3},{3,7},{12,8},{8,12},{13,... | collective-permute-start | bytes 1966088 | tf_op jit(solution)/shard_map/ppermute | solution.py:96
  349.2 49.6 %collective-permute-start.34 = (f32[320,256]{1,0:T(8,128)S(1)}, f32[320,256]{1,0:T(8,128)S(1)}, u32[]{:S(2)}, u32[]{:S(2)}) collective-permute-start(f32[320,256]{1,0:T(8,128)S(1)} %get-tuple-element.160), channel_id=1, source_target_pairs={{5,0},{1,1},{4,2},{0,3},{7,4},{3,5},{6,6},{2,7},{13,8},{9,9},{12,1... | collective-permute-start | bytes 983048 | tf_op jit(solution)/shard_map/ppermute | solution.py:160
  355.8 29.7 %collective-permute-start.37 = (f32[320,256]{1,0:T(8,128)S(1)}, f32[320,256]{1,0:T(8,128)S(1)}, u32[]{:S(2)}, u32[]{:S(2)}) collective-permute-start(f32[320,256]{1,0:T(8,128)S(1)} %get-tuple-element.161), channel_id=1, source_target_pairs={{0,0},{4,1},{1,2},{5,3},{2,4},{6,5},{3,6},{7,7},{8,8},{12,9},{9,10... | collective-permute-start | bytes 983048 | tf_op jit(solution)/shard_map/ppermute | solution.py:160
  356.4 29.0 %collective-permute-start.36 = (f32[320,256]{1,0:T(8,128)S(1)}, f32[320,256]{1,0:T(8,128)S(1)}, u32[]{:S(2)}, u32[]{:S(2)}) collective-permute-start(f32[320,256]{1,0:T(8,128)S(1)} %get-tuple-element.162), channel_id=1, source_target_pairs={{4,0},{0,1},{5,2},{1,3},{6,4},{2,5},{7,6},{3,7},{12,8},{8,9},{13,1... | collective-permute-start | bytes 983048 | tf_op jit(solution)/shard_map/ppermute | solution.py:160
  358.3 40.5 %collective-permute-start.35 = (f32[320,256]{1,0:T(8,128)S(1)}, f32[320,256]{1,0:T(8,128)S(1)}, u32[]{:S(2)}, u32[]{:S(2)}) collective-permute-start(f32[320,256]{1,0:T(8,128)S(1)} %get-tuple-element.163), channel_id=1, source_target_pairs={{1,0},{5,1},{0,2},{4,3},{3,4},{7,5},{2,6},{6,7},{9,8},{13,9},{8,10... | collective-permute-start | bytes 983048 | tf_op jit(solution)/shard_map/ppermute | solution.py:160
  396.1 30.4 %collective-permute-start.42 = (bf16[4,2,64,2048]{3,2,1,0:T(8,128)(2,1)S(1)}, bf16[4,2,64,2048]{3,2,1,0:T(8,128)(2,1)S(1)}, u32[]{:S(2)}, u32[]{:S(2)}) collective-permute-start(bf16[4,2,64,2048]{3,2,1,0:T(8,128)(2,1)S(1)} %fusion.24), channel_id=1, source_target_pairs={{0,8},{8,0},{16,24},{24,16},{1,9},{9,1},{17,25},{25,17},{2,10},{10... | collective-permute-start | bytes 6291464 | tf_op jit(solution)/shard_map/ppermute | solution.py:17
  432.6 29.3 %collective-permute-start.43 = (bf16[320,1024]{1,0:T(8,128)(2,1)S(1)}, bf16[320,1024]{1,0:T(8,128)(2,1)S(1)}, u32[]{:S(2)}, u32[]{:S(2)}) collective-permute-start(bf16[320,1024]{1,0:T(8,128)(2,1)S(1)} %copy-done.12), channel_id=1, source_target_pairs={{4,0},{0,4},{5,1},{1,5},{6,2},{2,6},{7,3},{3,7},{12,8},{8,12},{13,... | collective-permute-start | bytes 1966088 | tf_op jit(solution)/shard_map/ppermute | solution.py:96
  452.3 44.6 %collective-permute-start.47 = (bf16[4,1,64,2048]{3,2,0,1:T(8,128)(2,1)}, bf16[4,1,64,2048]{3,2,0,1:T(8,128)(2,1)}, u32[]{:S(2)}, u32[]{:S(2)}) collective-permute-start(bf16[4,1,64,2048]{3,2,0,1:T(8,128)(2,1)} %fusion.55), channel_id=1, source_target_pairs={{0,16},{8,24},{16,0},{24,8},{1,17},{9,25},{17,1},{25,9},{2,18},{10... | collective-permute-start | bytes 3145736 | tf_op jit(solution)/shard_map/ppermute | solution.py:17
  510.2 43.3 %collective-permute-start.55 = (bf16[320,1024]{1,0:T(8,128)(2,1)}, bf16[320,1024]{1,0:T(8,128)(2,1)}, u32[]{:S(2)}, u32[]{:S(2)}) collective-permute-start(bf16[320,1024]{1,0:T(8,128)(2,1)} %convolution_convert_fusion.6), channel_id=1, source_target_pairs={{0,4},{4,0},{1,5},{5,1},{2,6},{6,2},{3,7},{7,3},{8,12},{12,8},{9,1... | collective-permute-start | bytes 1966088 | tf_op jit(solution)/shard_map/ppermute | solution.py:108
  523.9 32.8 %collective-permute-start.49 = (bf16[4,2,64,1536]{3,2,0,1:T(8,128)(2,1)}, bf16[4,2,64,1536]{3,2,0,1:T(8,128)(2,1)}, u32[]{:S(2)}, u32[]{:S(2)}) collective-permute-start(bf16[4,2,64,1536]{3,2,0,1:T(8,128)(2,1)} %select_bitcast_fusion.4), channel_id=1, source_target_pairs={{0,8},{8,0},{16,24},{24,16},{1,9},{9,1},{17,25},{25,17},{2,10},{10... | collective-permute-start | bytes 4718600 | tf_op jit(solution)/shard_map/ppermute | solution.py:17
  (130 other events, 1521.6 us)

commit v3 on v2

--- a/solution.py
+++ b/solution.py
@@ -279,21 +279,21 @@
     here_row, here_col = lax.axis_index("row"), lax.axis_index("col")
     wide = w_qkv.shape[2]
     far, near = lax.axis_size("dp") // 2, 1
+    own_low = to_tokens(tokens.astype(jnp.bfloat16))
     qkv_held = gather_col(cut_piece(w_qkv.reshape(w_qkv.shape[0], 3 * wide)))
-    own_tokens = to_tokens(tokens)
     small = jnp.stack(
         [out_bias, down_bias, norm_gain[0], norm_gain[1], norm_bias[0], norm_bias[1]]
     )
     small = gather_small(small)
-    qkv_held, (piece_out, piece_up) = after(qkv_held, (cut_piece(w_out), cut_piece(w_up)))
-    out_held, up_held = gather_col(piece_out), gather_col(piece_up)
-    own_low = own_tokens.astype(jnp.bfloat16)
     other_low = from_others(own_low)
-    qkv_held, piece_down = after(gather_dp(qkv_held, far), cut_piece(w_down))
-    down_held = gather_col(piece_down)
-    qkv_held, (out_held, up_held) = after(gather_dp(qkv_held, near), (out_held, up_held))
+    pieces = jnp.concatenate([cut_piece(w_out), cut_piece(w_down)], 0)
+    (qkv_held, own_low), pieces = after((qkv_held, own_low), pieces)
+    pair_held = gather_col(pieces)
+    qkv_held, piece_up = after(gather_dp(qkv_held, far), cut_piece(w_up))
+    up_held = gather_col(piece_up)
+    qkv_held, pair_held = after(gather_dp(qkv_held, near), pair_held)
     w_qkv_all = whole_block(qkv_held).reshape(-1, 3 * wide)
-    out_held, up_held = gather_dp(out_held, far), gather_dp(up_held, far)
+    pair_held = gather_dp(pair_held, far)
     out_bias_all, down_bias_all = small[0], small[1]
     gains, shifts = small[2:4], small[4:6]
 
@@ -306,9 +306,8 @@
         ],
         0,
     )
-    qkv, (out_held, up_held, down_held) = after(qkv, (out_held, up_held, down_held))
-    out_held, down_held = gather_dp(out_held, near), gather_dp(down_held, far)
-    up_held = gather_dp(up_held, near)
+    qkv, (pair_held, up_held) = after(qkv, (pair_held, up_held))
+    pair_held, up_held = gather_dp(pair_held, near), gather_dp(up_held, far)
     length = qkv.shape[0]
     head_count = wide // HD
     qkv = qkv.reshape(length, 3, head_count, HD)
@@ -319,19 +318,20 @@
     same_seq = (segment[:, None] == segment[None, :])[None]
     context, log_total = attend(query_rows, key_rows, value_rows, same_seq, score_scale)
     context = context.reshape(length, wide).astype(jnp.bfloat16)
-    context, (down_held, cotangent) = after(context, (down_held, cotangent))
-    w_out_all = whole_block(out_held).transpose(1, 0, 2).reshape(w_out.shape[0], -1)
-    down_held = gather_dp(down_held, near)
+    context, (pair_held, up_held) = after(context, (pair_held, up_held))
+    cut = w_out.shape[0] // lax.axis_size("dp")
+    w_out_all = whole_block(pair_held[:, :, :cut]).transpose(1, 0, 2).reshape(w_out.shape[0], -1)
+    up_held = gather_dp(up_held, near)
     attn_other = dot(context[size:], w_out_all)
     attn_out = to_owners(attn_other, dot(context[:size], w_out_all)) + out_bias_all
-    normed_one, normal_one, inv_one = norm_forward(own_tokens + attn_out, gains[0], shifts[0])
+    normed_one, normal_one, inv_one = norm_forward(own_low.astype(jnp.float32) + attn_out, gains[0], shifts[0])
     normed_own = normed_one.astype(jnp.bfloat16)
-    normed_own, cotangent = after(normed_own, cotangent)
     normed_other = from_others(normed_own)
-    own_cotangent = to_tokens(cotangent)
     w_up_all = whole_block(up_held).reshape(-1, w_up.shape[1])
-    w_down_all = whole_block(down_held).transpose(1, 0, 2).reshape(w_down.shape[0], -1)
+    w_down_all = whole_block(pair_held[:, :, cut:]).transpose(1, 0, 2).reshape(w_down.shape[0], -1)
     pre_own = dot(normed_own, w_up_all) + up_bias
+    pre_own, cotangent_low = after(pre_own, cotangent.astype(jnp.bfloat16))
+    own_cotangent = to_tokens(cotangent_low).astype(jnp.float32)
     pre_other = dot(normed_other, w_up_all) + up_bias
     hidden_own = gelu_exact(pre_own).astype(jnp.bfloat16)
     hidden_other = gelu_exact(pre_other).astype(jnp.bfloat16)
@@ -346,7 +346,7 @@
     mlp_grad_other = from_others(mlp_grad_own)
     down_total = jnp.sum(mlp_grad_own, 0, dtype=jnp.float32)
     mlp_grad_own, last = after(mlp_grad_own, last)
-    output = from_tokens(last)
+    output = from_tokens(last.astype(jnp.bfloat16)).astype(jnp.float32)
     down_sum = cut_grad(outer_blocks(hidden, jnp.concatenate([mlp_grad_own, mlp_grad_other], 0)))
     down_sum = halve_dp(down_sum, near)
     pre_grad_own = jax.vjp(gelu_exact, pre_own)[1](dot_back(mlp_grad_own, w_down_all))[0]
@@ -372,7 +372,7 @@
     out_total = jnp.sum(attn_grad_own, 0, dtype=jnp.float32)
     totals = add_up(
         jnp.stack([out_total, down_total, gain_one, gain_two, shift_one, shift_two]),
-        ("row", "col", "dp"),
+        ("row",),
     )
     grad_context = jnp.concatenate(
         [
@@ -399,16 +399,12 @@
     up_sum = scatter_col(up_sum)
     down_sum = gather_dp(down_sum, far)
     input_other = dot_back(grad_qkv[size:], w_qkv_all)
-    halves = add_up(
-        jnp.concatenate([up_total, qkv_totals[:wide], qkv_totals[2 * wide :]])[None],
-        ("col", "dp"),
-    )[0]
     grad_own = to_owners(input_other, dot_back(grad_qkv[:size], w_qkv_all)) + grad_middle
     qkv_sum, (out_sum, up_sum, down_sum, grad_own) = after(
         qkv_sum, (out_sum, up_sum, down_sum, grad_own)
     )
     qkv_sum = halve_dp(qkv_sum, far)
-    grad_input = from_tokens(grad_own)
+    grad_input = from_tokens(grad_own.astype(jnp.bfloat16)).astype(jnp.float32)
     out_sum = scatter_col(out_sum)
     up_sum = gather_dp(up_sum, far)
     down_sum = gather_dp(down_sum, near)
@@ -421,6 +417,12 @@
     out_sum = gather_dp(out_sum, near)
     qkv_sum = gather_dp(qkv_sum, near)
 
+    sums = jnp.concatenate(
+        [totals.reshape(-1), up_total, qkv_totals[:wide], qkv_totals[2 * wide :]]
+    )
+    sums = add_up(sums.reshape(-1, 128), ("dp", "col")).reshape(-1)
+    halves = sums[totals.size :]
+    totals = sums[: totals.size].reshape(totals.shape)
     part = totals.shape[1] // cols
     mine = lax.dynamic_slice_in_dim(totals, here_col * part, part, 1)
     hid = up_total.shape[0]

time: 657 us -> 579 us (0.88)
  waiting for transfers between devices: 257 us -> 180 us
    ppermute x8, waiting for transfers between devices: 55.7 us -> 10.4 us  [to_tokens(): got.append(lax.ppermute(give, ('row', 'col'), owner_perm(rows, cols, k)))]
    ppermute x59 -> x50, starting transfers between devices: 149 us -> 105 us  [hop(): return lax.ppermute(values, axis, [(i, i ^ step) for i in range(count)])]
    ppermute x8, starting transfers between devices: 22.2 us -> 57.7 us  [to_tokens(): got.append(lax.ppermute(give, ('row', 'col'), owner_perm(rows, cols, k)))]
    ppermute x59 -> x50, waiting for transfers between devices: 169 us -> 150 us  [hop(): return lax.ppermute(values, axis, [(i, i ^ step) for i in range(count)])]
    convert_element_type x1 -> x5, other arithmetic: 0.08 us -> 11.6 us  [the longest x1 5.6 us: shards(): hidden_own = gelu_exact(pre_own).astype(jnp.bfloat16)]
    ppermute x4, starting transfers between devices: 4.48 us -> 12.5 us  [to_owners(): lax.ppermute(low[(k - 1) * size:k * size], 'row', [(i, (i + k) % count) f...]
    dot_general x8, matrix products: 28.9 us -> 21 us  [dot(): return jnp.dot(first, second, preferred_element_type=jnp.float32)]
    reshape x0 -> x4, local copies, waits for them, and re-layouts: none -> 7.82 us  [the longest x2 7.8 us: whole_block(): held.reshape((held.shape[0], held.shape[1] * held.shape[2]) + held.shape[...]
  transfers between devices with their start and end apart: 83 -> 74, of which waited for: 34 -> 29; matrix products, arithmetic and copies ran while one was open for 22% -> 26% of each run, Pallas kernels for 0% -> 0%
where the time goes in v3:
time: 579 us; the launch traced here: 575 us
  starting transfers between devices  202 us (35%)
  waiting for transfers between devices  180 us (31%)
  matrix products  78.6 us (14%)
  other arithmetic  64 us (11%)
  local copies, waits for them, and re-layouts  48.6 us (8%)
    ppermute x50, waiting for transfers between devices, hop(): return lax.ppermute(values, axis, [(i, i ^ step) for i in range(count)])  150 us
    ppermute x50, starting transfers between devices, hop(): return lax.ppermute(values, axis, [(i, i ^ step) for i in range(count)])  105 us
    ppermute x8, starting transfers between devices, to_tokens(): got.append(lax.ppermute(give, ('row', 'col'), owner_perm(rows, cols, k)))  57.7 us
    ppermute x8, starting transfers between devices, from_tokens(): got.append(lax.ppermute(give, ('row', 'col'), back))  21.6 us
    dot_general x8, matrix products, dot(): return jnp.dot(first, second, preferred_element_type=jnp.float32)  21 us
    dot_general x10, matrix products, outer(): jnp.einsum('td,tf->df', first, second, preferred_element_type=jnp.float32)  17.7 us
    dot_general x8, matrix products, dot_back(): jnp.einsum('tf,df->td', first, second, preferred_element_type=jnp.float32)  16.1 us
    another operation x36, other arithmetic, in_order(): jnp.stack([jnp.where(flag, theirs, mine), jnp.where(flag, mine, theirs)],...  13.8 us
  transfers between devices with their start and end apart: 74, of which 29 were waited for; matrix products, arithmetic and copies ran while one was open for 26% of the time, Pallas kernels for 0%

profile of v3, /device:TPU:1, one launch (start us, length us, event | category | flops | bytes accessed | tf_op | source)
XLA Modules:
  0.0 575.0 jit_solution(1850267037360955466)
XLA Ops:
  17.0 44.6 %collective-permute-start.3 = (bf16[320,256]{1,0:T(8,128)(2,1)}, bf16[320,256]{1,0:T(8,128)(2,1)S(1)}, u32[]{:S(2)}, u32[]{:S(2)}) collective-permute-start(bf16[320,256]{1,0:T(8,128)(2,1)} %get-tuple-element.193), channel_id=1, source_target_pairs={{0,5},{1,1},{2,4},{3,0},{4,7},{5,3},{6,6},{7,2},{8,13},{9,9},{10,1... | collective-permute-start | bytes 491528 | tf_op jit(solution)/shard_map/ppermute | solution.py:133
  82.4 7.6 %collective-permute-done.7 = bf16[4,1,64,1536]{3,2,0,1:T(8,128)(2,1)S(1)} collective-permute-done((bf16[4,1,64,1536]{3,2,0,1:T(8,128)(2,1)S(1)}, bf16[4,1,64,1536]{3,2,0,1:T(8,128)(2,1)S(1)}, u32[]{:S(2)}, u32[]{:S(2)}) %collective-permute-start.7) | collective-permute-done | bytes 786464 | tf_op jit(solution)/shard_map/ppermute | solution.py:17
  98.1 9.6 %collective-permute-start.16 = (bf16[64,2048]{1,0:T(8,128)(2,1)S(1)}, bf16[64,2048]{1,0:T(8,128)(2,1)S(1)}, u32[]{:S(2)}, u32[]{:S(2)}) collective-permute-start(bf16[64,2048]{1,0:T(8,128)(2,1)S(1)} %dynamic-slice_convert_fusion.1), channel_id=1, source_target_pairs={{0,1},{1,0},{2,3},{3,2},{4,5},{5,4},{6,7},{7,6},{8,9},{9,8},{10,11... | collective-permute-start | bytes 786440 | tf_op jit(solution)/shard_map/ppermute | solution.py:17
  115.5 9.2 %collective-permute-done.14 = bf16[64,2048]{1,0:T(8,128)(2,1)S(1)} collective-permute-done((bf16[64,2048]{1,0:T(8,128)(2,1)S(1)}, bf16[64,2048]{1,0:T(8,128)(2,1)S(1)}, u32[]{:S(2)}, u32[]{:S(2)}) %collective-permute-start.14) | collective-permute-done | bytes 262176 | tf_op jit(solution)/shard_map/ppermute | solution.py:17
  130.9 17.7 %collective-permute-done.13 = bf16[4,1,640,256]{3,2,0,1:T(8,128)(2,1)S(1)} collective-permute-done((bf16[4,1,640,256]{3,2,0,1:T(8,128)(2,1)S(1)}, bf16[4,1,640,256]{3,2,0,1:T(8,128)(2,1)S(1)}, u32[]{:S(2)}, u32[]{:S(2)}) %collective-permute-start.13) | collective-permute-done | bytes 1310752 | tf_op jit(solution)/shard_map/ppermute | solution.py:17
  153.6 8.3 %collective-permute-start.17 = (bf16[4,2,640,256]{3,2,1,0:T(8,128)(2,1)}, bf16[4,2,640,256]{3,2,1,0:T(8,128)(2,1)}, u32[]{:S(2)}, u32[]{:S(2)}) collective-permute-start(bf16[4,2,640,256]{3,2,1,0:T(8,128)(2,1)} %maximum_bitcast_fusion), channel_id=1, source_target_pairs={{0,8},{8,0},{16,24},{24,16},{1,9},{9,1},{17,25},{25,17},{2,10},{10... | collective-permute-start | bytes 7864328 | tf_op jit(solution)/shard_map/ppermute | solution.py:17
  178.8 6.9 %collective-permute-start.22 = (bf16[4,2,64,2048]{3,2,1,0:T(8,128)(2,1)S(1)}, bf16[4,2,64,2048]{3,2,1,0:T(8,128)(2,1)}, u32[]{:S(2)}, u32[]{:S(2)}) collective-permute-start(bf16[4,2,64,2048]{3,2,1,0:T(8,128)(2,1)S(1)} %maximum_bitcast_fusion.1), channel_id=1, source_target_pairs={{0,8},{8,0},{16,24},{24,16},{1,9},{9,1},{17,25},{25,17},{2,10},{10... | collective-permute-start | bytes 6291464 | tf_op jit(solution)/shard_map/ppermute | solution.py:17
  185.7 12.0 %collective-permute-start.20 = (f32[6,256]{1,0:T(8,128)S(1)}, f32[6,256]{1,0:T(8,128)S(1)}, u32[]{:S(2)}, u32[]{:S(2)}) collective-permute-start(f32[6,256]{1,0:T(8,128)S(1)} %pad_maximum_fusion.35), channel_id=1, source_target_pairs={{0,1},{1,0},{2,3},{3,2},{4,5},{5,4},{6,7},{7,6},{8,9},{9,8},{10,11... | collective-permute-start | bytes 18440 | tf_op jit(solution)/shard_map/ppermute | solution.py:17
  213.8 6.3 %copy.132 = bf16[4,2048,256]{1,2,0:T(8,128)(2,1)} copy(bf16[4,2048,256]{2,1,0:T(8,128)(2,1)} %bitcast.494) | data formatting | bytes 8388608 | tf_op jit(solution)/shard_map/reshape | solution.py:57
  237.8 8.2 %multiply_convert_fusion.1 = (bf16[320,2048]{1,0:T(8,128)(2,1)S(1)}, f32[320,2048]{1,0:T(8,128)S(1)}, f32[320,2048]{1,0:T(8,128)S(1)}) fusion(f32[2048]{0:T(1024)S(1)} %copy-done.38, bf16[320,1024]{1,0:T(8,128)(2,1)S(1)} %collective-permute-done.23, bf16[1024,2048]{1,0:T(8,128)(2,1)S(1)} %bitcast.514), kind=kOutput, calls=%fused_computation.42 | convolution fusion | flops 1385431040 | bytes 11411456 | tf_op jit(solution)/shard_map/dot_general | solution.py:207
  265.1 6.5 %collective-permute-start.29 = (bf16[320,256]{1,0:T(8,128)(2,1)S(1)}, bf16[320,256]{1,0:T(8,128)(2,1)S(1)}, u32[]{:S(2)}, u32[]{:S(2)}) collective-permute-start(bf16[320,256]{1,0:T(8,128)(2,1)S(1)} %get-tuple-element.177), channel_id=1, source_target_pairs={{5,0},{1,1},{4,2},{0,3},{7,4},{3,5},{6,6},{2,7},{13,8},{9,9},{12,1... | collective-permute-start | bytes 491528 | tf_op jit(solution)/shard_map/ppermute | solution.py:160
  282.8 14.8 %collective-permute-start.34 = (bf16[4,2,512,256]{3,2,1,0:T(8,128)(2,1)S(1)}, bf16[4,2,512,256]{3,2,1,0:T(8,128)(2,1)S(1)}, u32[]{:S(2)}, u32[]{:S(2)}) collective-permute-start(bf16[4,2,512,256]{3,2,1,0:T(8,128)(2,1)S(1)} %fusion.23), channel_id=1, source_target_pairs={{0,8},{8,0},{16,24},{24,16},{1,9},{9,1},{17,25},{25,17},{2,10},{10... | collective-permute-start | bytes 6291464 | tf_op jit(solution)/shard_map/ppermute | solution.py:17
  312.8 6.8 %collective-permute-start.35 = (bf16[320,1024]{1,0:T(8,128)(2,1)S(1)}, bf16[320,1024]{1,0:T(8,128)(2,1)S(1)}, u32[]{:S(2)}, u32[]{:S(2)}) collective-permute-start(bf16[320,1024]{1,0:T(8,128)(2,1)S(1)} %convolution_convert_fusion.7), channel_id=1, source_target_pairs={{0,4},{4,0},{1,5},{5,1},{2,6},{6,2},{3,7},{7,3},{8,12},{12,8},{9,1... | collective-permute-start | bytes 1966088 | tf_op jit(solution)/shard_map/ppermute | solution.py:108
  325.8 8.2 %collective-permute-done.35 = bf16[320,1024]{1,0:T(8,128)(2,1)S(1)} collective-permute-done((bf16[320,1024]{1,0:T(8,128)(2,1)S(1)}, bf16[320,1024]{1,0:T(8,128)(2,1)S(1)}, u32[]{:S(2)}, u32[]{:S(2)}) %collective-permute-start.35) | collective-permute-done | bytes 655392 | tf_op jit(solution)/shard_map/ppermute | solution.py:108
  337.9 12.0 %collective-permute-done.36 = bf16[4,1,512,256]{3,2,0,1:T(8,128)(2,1)S(1)} collective-permute-done((bf16[4,1,512,256]{3,2,0,1:T(8,128)(2,1)S(1)}, bf16[4,1,512,256]{3,2,0,1:T(8,128)(2,1)S(1)}, u32[]{:S(2)}, u32[]{:S(2)}) %collective-permute-start.36) | collective-permute-done | bytes 1048608 | tf_op jit(solution)/shard_map/ppermute | solution.py:17
  360.4 9.0 %collective-permute-done.66 = f32[6,1024]{1,0:T(8,128)S(1)} collective-permute-done((f32[6,1024]{1,0:T(8,128)S(1)}, f32[6,1024]{1,0:T(8,128)S(1)}, u32[]{:S(2)}, u32[]{:S(2)}) %collective-permute-start.66) | collective-permute-done | bytes 24608 | tf_op jit(solution)/shard_map/ppermute | solution.py:17
  369.7 9.4 %collective-permute-done.40 = bf16[1,512,256]{2,1,0:T(8,128)(2,1)} collective-permute-done((bf16[1,512,256]{2,1,0:T(8,128)(2,1)}, bf16[1,512,256]{2,1,0:T(8,128)(2,1)}, u32[]{:S(2)}, u32[]{:S(2)}) %collective-permute-start.40) | collective-permute-done | bytes 262176 | tf_op jit(solution)/shard_map/ppermute | solution.py:17
  389.3 12.4 %multiply_reduce_fusion = (f32[8,640]{1,0:T(8,128)S(1)}, f32[8,640,640]{1,2,0:T(8,128)}) fusion(f32[8,640,640]{1,2,0:T(8,128)} %copy-done.2, f32[8,640]{1,0:T(8,128)S(1)} %log_add_fusion, bf16[640,8,64]{0,2,1:T(8,128)(2,1)S(1)} %bitcast.507, bf16[640,3,8,64]{0,3,2,1:T(8,128)(2,1)} %bitcast.497), kind=kOutput, calls=%fused_computation.1 | convolution fusion | flops 429255680 | bytes 27566080 | tf_op jit(solution)/shard_map/qhe,khe->hqk/dot_general | solution.py:239
  401.7 6.8 %multiply_convert_fusion = bf16[8,640,640]{1,2,0:T(8,128)(2,1)S(1)} fusion(f32[8,640,640]{1,2,0:T(8,128)} %get-tuple-element.257, f32[8,640,640]{1,2,0:T(8,128)S(1)} %bitcast.485, f32[8,640]{1,0:T(8,128)S(1)} %get-tuple-element.256, f32[8,640]{1,0:T(8,128)S(1)} %log_add_fusion), kind=kLoop, calls=%fused_computation | loop fusion | flops 13107200 | bytes 32808960 | tf_op jit(solution)/shard_map/convert_element_type | solution.py:249
  431.4 7.4 %collective-permute-done.68 = f32[72,128]{1,0:T(8,128)S(1)} collective-permute-done((f32[72,128]{1,0:T(8,128)S(1)}, f32[72,128]{1,0:T(8,128)S(1)}, u32[]{:S(2)}, u32[]{:S(2)}) %collective-permute-start.68) | collective-permute-done | bytes 36896 | tf_op jit(solution)/shard_map/ppermute | solution.py:17
  462.0 16.4 %collective-permute-done.47 = bf16[1,64,2048]{2,1,0:T(8,128)(2,1)S(1)} collective-permute-done((bf16[1,64,2048]{2,1,0:T(8,128)(2,1)}, bf16[1,64,2048]{2,1,0:T(8,128)(2,1)S(1)}, u32[]{:S(2)}, u32[]{:S(2)}) %collective-permute-start.47) | collective-permute-done | bytes 262176 | tf_op jit(solution)/shard_map/ppermute | solution.py:17
  497.2 7.5 %collective-permute-start.52 = (bf16[320,256]{1,0:T(8,128)(2,1)S(1)}, bf16[320,256]{1,0:T(8,128)(2,1)S(1)}, u32[]{:S(2)}, u32[]{:S(2)}) collective-permute-start(bf16[320,256]{1,0:T(8,128)(2,1)S(1)} %get-tuple-element.173), channel_id=1, source_target_pairs={{1,0},{5,1},{0,2},{4,3},{3,4},{7,5},{2,6},{6,7},{9,8},{13,9},{8,10... | collective-permute-start | bytes 491528 | tf_op jit(solution)/shard_map/ppermute | solution.py:160
  512.4 16.6 %collective-permute-done.55 = bf16[4,1,64,1536]{3,2,1,0:T(8,128)(2,1)S(1)} collective-permute-done((bf16[4,1,64,1536]{3,2,1,0:T(8,128)(2,1)S(1)}, bf16[4,1,64,1536]{3,2,1,0:T(8,128)(2,1)S(1)}, u32[]{:S(2)}, u32[]{:S(2)}) %collective-permute-start.55) | collective-permute-done | bytes 786464 | tf_op jit(solution)/shard_map/ppermute | solution.py:17
  543.3 9.8 %collective-permute-done.61 = bf16[1,64,1536]{2,1,0:T(8,128)(2,1)S(1)} collective-permute-done((bf16[1,64,1536]{2,1,0:T(8,128)(2,1)S(1)}, bf16[1,64,1536]{2,1,0:T(8,128)(2,1)S(1)}, u32[]{:S(2)}, u32[]{:S(2)}) %collective-permute-start.61) | collective-permute-done | bytes 196640 | tf_op jit(solution)/shard_map/ppermute | solution.py:17
  (405 shorter events, 298.6 us)
Async XLA Ops:
  3.4 66.9 %collective-permute-start.2 = (bf16[64,1536]{0,1:T(8,128)(2,1)}, bf16[64,1536]{0,1:T(8,128)(2,1)}, u32[]{:S(2)}, u32[]{:S(2)}) collective-permute-start(bf16[64,1536]{0,1:T(8,128)(2,1)} %dynamic-slice_convert_fusion), channel_id=1, source_target_pairs={{0,1},{1,0},{2,3},{3,2},{4,5},{5,4},{6,7},{7,6},{8,9},{9,8},{10,11... | collective-permute-start | bytes 589832 | tf_op jit(solution)/shard_map/ppermute | solution.py:17
  5.6 66.0 %collective-permute-start.1 = (bf16[64,1536]{0,1:T(8,128)(2,1)}, bf16[64,1536]{0,1:T(8,128)(2,1)}, u32[]{:S(2)}, u32[]{:S(2)}) collective-permute-start(bf16[64,1536]{0,1:T(8,128)(2,1)} %dynamic-slice_convert_fusion), channel_id=1, source_target_pairs={{0,2},{1,3},{2,0},{3,1},{4,6},{5,7},{6,4},{7,5},{8,10},{9,11},{10,... | collective-permute-start | bytes 589832 | tf_op jit(solution)/shard_map/ppermute | solution.py:17
  7.9 63.7 %collective-permute-start = (bf16[64,1536]{0,1:T(8,128)(2,1)}, bf16[64,1536]{0,1:T(8,128)(2,1)}, u32[]{:S(2)}, u32[]{:S(2)}) collective-permute-start(bf16[64,1536]{0,1:T(8,128)(2,1)} %dynamic-slice_convert_fusion), channel_id=1, source_target_pairs={{0,3},{1,2},{2,1},{3,0},{4,7},{5,6},{6,5},{7,4},{8,11},{9,10},{10,... | collective-permute-start | bytes 589832 | tf_op jit(solution)/shard_map/ppermute | solution.py:17
  11.7 49.9 %collective-permute-start.5 = (bf16[320,256]{1,0:T(8,128)(2,1)}, bf16[320,256]{1,0:T(8,128)(2,1)S(1)}, u32[]{:S(2)}, u32[]{:S(2)}) collective-permute-start(bf16[320,256]{1,0:T(8,128)(2,1)} %get-tuple-element.195), channel_id=1, source_target_pairs={{0,4},{1,0},{2,5},{3,1},{4,6},{5,2},{6,7},{7,3},{8,12},{9,8},{10,1... | collective-permute-start | bytes 491528 | tf_op jit(solution)/shard_map/ppermute | solution.py:133
  17.0 47.5 %collective-permute-start.3 = (bf16[320,256]{1,0:T(8,128)(2,1)}, bf16[320,256]{1,0:T(8,128)(2,1)S(1)}, u32[]{:S(2)}, u32[]{:S(2)}) collective-permute-start(bf16[320,256]{1,0:T(8,128)(2,1)} %get-tuple-element.193), channel_id=1, source_target_pairs={{0,5},{1,1},{2,4},{3,0},{4,7},{5,3},{6,6},{7,2},{8,13},{9,9},{10,1... | collective-permute-start | bytes 491528 | tf_op jit(solution)/shard_map/ppermute | solution.py:133
  76.8 51.4 %collective-permute-start.12 = (bf16[320,1024]{1,0:T(8,128)(2,1)}, bf16[320,1024]{1,0:T(8,128)(2,1)S(1)}, u32[]{:S(2)}, u32[]{:S(2)}) collective-permute-start(bf16[320,1024]{1,0:T(8,128)(2,1)} %pad_maximum_fusion.15), channel_id=1, source_target_pairs={{4,0},{0,4},{5,1},{1,5},{6,2},{2,6},{7,3},{3,7},{12,8},{8,12},{13,... | collective-permute-start | bytes 1966088 | tf_op jit(solution)/shard_map/ppermute | solution.py:96
  90.3 34.5 %collective-permute-start.8 = (bf16[4,2,64,1536]{3,2,1,0:T(8,128)(2,1)S(1)}, bf16[4,2,64,1536]{3,2,1,0:T(8,128)(2,1)S(1)}, u32[]{:S(2)}, u32[]{:S(2)}) collective-permute-start(bf16[4,2,64,1536]{3,2,1,0:T(8,128)(2,1)S(1)} %maximum_bitcast_fusion.2), channel_id=1, source_target_pairs={{0,8},{8,0},{16,24},{24,16},{1,9},{9,1},{17,25},{25,17},{2,10},{10... | collective-permute-start | bytes 4718600 | tf_op jit(solution)/shard_map/ppermute | solution.py:17
  178.8 45.1 %collective-permute-start.22 = (bf16[4,2,64,2048]{3,2,1,0:T(8,128)(2,1)S(1)}, bf16[4,2,64,2048]{3,2,1,0:T(8,128)(2,1)}, u32[]{:S(2)}, u32[]{:S(2)}) collective-permute-start(bf16[4,2,64,2048]{3,2,1,0:T(8,128)(2,1)S(1)} %maximum_bitcast_fusion.1), channel_id=1, source_target_pairs={{0,8},{8,0},{16,24},{24,16},{1,9},{9,1},{17,25},{25,17},{2,10},{10... | collective-permute-start | bytes 6291464 | tf_op jit(solution)/shard_map/ppermute | solution.py:17
  228.1 27.6 %collective-permute-start.25 = (bf16[320,256]{1,0:T(8,128)(2,1)S(1)}, bf16[320,256]{1,0:T(8,128)(2,1)S(1)}, u32[]{:S(2)}, u32[]{:S(2)}) collective-permute-start(bf16[320,256]{1,0:T(8,128)(2,1)S(1)} %get-tuple-element.183), channel_id=1, source_target_pairs={{0,5},{1,1},{2,4},{3,0},{4,7},{5,3},{6,6},{7,2},{8,13},{9,9},{10,1... | collective-permute-start | bytes 491528 | tf_op jit(solution)/shard_map/ppermute | solution.py:133
  231.5 24.1 %collective-permute-start.28 = (bf16[320,256]{1,0:T(8,128)(2,1)S(1)}, bf16[320,256]{1,0:T(8,128)(2,1)S(1)}, u32[]{:S(2)}, u32[]{:S(2)}) collective-permute-start(bf16[320,256]{1,0:T(8,128)(2,1)S(1)} %get-tuple-element.184), channel_id=1, source_target_pairs={{0,0},{1,4},{2,1},{3,5},{4,2},{5,6},{6,3},{7,7},{8,8},{9,12},{10,9... | collective-permute-start | bytes 491528 | tf_op jit(solution)/shard_map/ppermute | solution.py:133
  235.6 24.5 %collective-permute-start.26 = (bf16[320,256]{1,0:T(8,128)(2,1)S(1)}, bf16[320,256]{1,0:T(8,128)(2,1)S(1)}, u32[]{:S(2)}, u32[]{:S(2)}) collective-permute-start(bf16[320,256]{1,0:T(8,128)(2,1)S(1)} %get-tuple-element.186), channel_id=1, source_target_pairs={{0,1},{1,5},{2,0},{3,4},{4,3},{5,7},{6,2},{7,6},{8,9},{9,13},{10,8... | collective-permute-start | bytes 491528 | tf_op jit(solution)/shard_map/ppermute | solution.py:133
  265.1 36.8 %collective-permute-start.29 = (bf16[320,256]{1,0:T(8,128)(2,1)S(1)}, bf16[320,256]{1,0:T(8,128)(2,1)S(1)}, u32[]{:S(2)}, u32[]{:S(2)}) collective-permute-start(bf16[320,256]{1,0:T(8,128)(2,1)S(1)} %get-tuple-element.177), channel_id=1, source_target_pairs={{5,0},{1,1},{4,2},{0,3},{7,4},{3,5},{6,6},{2,7},{13,8},{9,9},{12,1... | collective-permute-start | bytes 491528 | tf_op jit(solution)/shard_map/ppermute | solution.py:160
  271.6 30.3 %collective-permute-start.30 = (bf16[320,256]{1,0:T(8,128)(2,1)S(1)}, bf16[320,256]{1,0:T(8,128)(2,1)S(1)}, u32[]{:S(2)}, u32[]{:S(2)}) collective-permute-start(bf16[320,256]{1,0:T(8,128)(2,1)S(1)} %get-tuple-element.179), channel_id=1, source_target_pairs={{1,0},{5,1},{0,2},{4,3},{3,4},{7,5},{2,6},{6,7},{9,8},{13,9},{8,10... | collective-permute-start | bytes 491528 | tf_op jit(solution)/shard_map/ppermute | solution.py:160
  282.8 27.5 %collective-permute-start.34 = (bf16[4,2,512,256]{3,2,1,0:T(8,128)(2,1)S(1)}, bf16[4,2,512,256]{3,2,1,0:T(8,128)(2,1)S(1)}, u32[]{:S(2)}, u32[]{:S(2)}) collective-permute-start(bf16[4,2,512,256]{3,2,1,0:T(8,128)(2,1)S(1)} %fusion.23), channel_id=1, source_target_pairs={{0,8},{8,0},{16,24},{24,16},{1,9},{9,1},{17,25},{25,17},{2,10},{10... | collective-permute-start | bytes 6291464 | tf_op jit(solution)/shard_map/ppermute | solution.py:17
  323.8 26.5 %collective-permute-start.37 = (bf16[4,2,64,2048]{3,2,1,0:T(8,128)(2,1)S(1)}, bf16[4,2,64,2048]{3,2,1,0:T(8,128)(2,1)S(1)}, u32[]{:S(2)}, u32[]{:S(2)}) collective-permute-start(bf16[4,2,64,2048]{3,2,1,0:T(8,128)(2,1)S(1)} %fusion.24), channel_id=1, source_target_pairs={{0,8},{8,0},{16,24},{24,16},{1,9},{9,1},{17,25},{25,17},{2,10},{10... | collective-permute-start | bytes 6291464 | tf_op jit(solution)/shard_map/ppermute | solution.py:17
  325.0 24.8 %collective-permute-start.36 = (bf16[4,1,512,256]{3,2,0,1:T(8,128)(2,1)S(1)}, bf16[4,1,512,256]{3,2,0,1:T(8,128)(2,1)S(1)}, u32[]{:S(2)}, u32[]{:S(2)}) collective-permute-start(bf16[4,1,512,256]{3,2,0,1:T(8,128)(2,1)S(1)} %fusion.60), channel_id=1, source_target_pairs={{0,16},{8,24},{16,0},{24,8},{1,17},{9,25},{17,1},{25,9},{2,18},{10... | collective-permute-start | bytes 3145736 | tf_op jit(solution)/shard_map/ppermute | solution.py:17
  353.1 28.0 %collective-permute-start.38 = (bf16[320,1024]{1,0:T(8,128)(2,1)S(1)}, bf16[320,1024]{1,0:T(8,128)(2,1)S(1)}, u32[]{:S(2)}, u32[]{:S(2)}) collective-permute-start(bf16[320,1024]{1,0:T(8,128)(2,1)S(1)} %get-tuple-element.67), channel_id=1, source_target_pairs={{4,0},{0,4},{5,1},{1,5},{6,2},{2,6},{7,3},{3,7},{12,8},{8,12},{13,... | collective-permute-start | bytes 1966088 | tf_op jit(solution)/shard_map/ppermute | solution.py:96
  355.4 23.7 %collective-permute-start.40 = (bf16[1,512,256]{2,1,0:T(8,128)(2,1)}, bf16[1,512,256]{2,1,0:T(8,128)(2,1)}, u32[]{:S(2)}, u32[]{:S(2)}) collective-permute-start(bf16[1,512,256]{2,1,0:T(8,128)(2,1)} %get-tuple-element.157), channel_id=1, source_target_pairs={{0,2},{1,3},{2,0},{3,1},{4,6},{5,7},{6,4},{7,5},{8,10},{9,11},{10,... | collective-permute-start | bytes 786440 | tf_op jit(solution)/shard_map/ppermute | solution.py:17
  369.4 47.5 %collective-permute-start.42 = (bf16[4,1,64,2048]{3,2,0,1:T(8,128)(2,1)}, bf16[4,1,64,2048]{3,2,0,1:T(8,128)(2,1)}, u32[]{:S(2)}, u32[]{:S(2)}) collective-permute-start(bf16[4,1,64,2048]{3,2,0,1:T(8,128)(2,1)} %fusion.61), channel_id=1, source_target_pairs={{0,16},{8,24},{16,0},{24,8},{1,17},{9,25},{17,1},{25,9},{2,18},{10... | collective-permute-start | bytes 3145736 | tf_op jit(solution)/shard_map/ppermute | solution.py:17
  424.8 29.8 %collective-permute-start.45 = (bf16[4,1,128,256]{3,2,0,1:T(8,128)(2,1)}, bf16[4,1,128,256]{3,2,0,1:T(8,128)(2,1)}, u32[]{:S(2)}, u32[]{:S(2)}) collective-permute-start(bf16[4,1,128,256]{3,2,0,1:T(8,128)(2,1)} %fusion.91), channel_id=1, source_target_pairs={{0,16},{8,24},{16,0},{24,8},{1,17},{9,25},{17,1},{25,9},{2,18},{10... | collective-permute-start | bytes 786440 | tf_op jit(solution)/shard_map/ppermute | solution.py:17
  425.0 27.0 %collective-permute-start.49 = (bf16[1,1,512,256]{3,2,1,0:T(8,128)(2,1)S(1)}, bf16[1,1,512,256]{3,2,1,0:T(8,128)(2,1)}, u32[]{:S(2)}, u32[]{:S(2)}) collective-permute-start(bf16[1,1,512,256]{3,2,1,0:T(8,128)(2,1)S(1)} %copy-done.20), channel_id=1, source_target_pairs={{0,16},{8,24},{16,0},{24,8},{1,17},{9,25},{17,1},{25,9},{2,18},{10... | collective-permute-start | bytes 786440 | tf_op jit(solution)/shard_map/ppermute | solution.py:17
  426.2 53.2 %collective-permute-start.50 = (bf16[320,1024]{1,0:T(8,128)(2,1)}, bf16[320,1024]{1,0:T(8,128)(2,1)}, u32[]{:S(2)}, u32[]{:S(2)}) collective-permute-start(bf16[320,1024]{1,0:T(8,128)(2,1)} %convolution_convert_fusion.6), channel_id=1, source_target_pairs={{0,4},{4,0},{1,5},{5,1},{2,6},{6,2},{3,7},{7,3},{8,12},{12,8},{9,1... | collective-permute-start | bytes 1966088 | tf_op jit(solution)/shard_map/ppermute | solution.py:108
  446.5 36.3 %collective-permute-start.44 = (bf16[4,2,64,1536]{3,2,0,1:T(8,128)(2,1)}, bf16[4,2,64,1536]{3,2,0,1:T(8,128)(2,1)}, u32[]{:S(2)}, u32[]{:S(2)}) collective-permute-start(bf16[4,2,64,1536]{3,2,0,1:T(8,128)(2,1)} %select_bitcast_fusion.4), channel_id=1, source_target_pairs={{0,8},{8,0},{16,24},{24,16},{1,9},{9,1},{17,25},{25,17},{2,10},{10... | collective-permute-start | bytes 4718600 | tf_op jit(solution)/shard_map/ppermute | solution.py:17
  454.5 23.8 %collective-permute-start.47 = (bf16[1,64,2048]{2,1,0:T(8,128)(2,1)}, bf16[1,64,2048]{2,1,0:T(8,128)(2,1)S(1)}, u32[]{:S(2)}, u32[]{:S(2)}) collective-permute-start(bf16[1,64,2048]{2,1,0:T(8,128)(2,1)} %get-tuple-element.154), channel_id=1, source_target_pairs={{0,2},{1,3},{2,0},{3,1},{4,6},{5,7},{6,4},{7,5},{8,10},{9,11},{10,... | collective-permute-start | bytes 786440 | tf_op jit(solution)/shard_map/ppermute | solution.py:17
  (94 other events, 935.0 us)
